TPU v7x, 512 devices: a whole 4x4x16 slice. The times are simulated.
512 devices in a mesh: fibre: 128 (over y_lo, z, x), win: 4 (over y_hi, core).
Axes of the slice: x: 4, y: 4 (y_hi: 2, y_lo: 2; y = y_hi * 2 + y_lo), z: 16, core: 2. Of those that a mesh axis runs over, the one named last changes fastest.
Arguments:
- samples_data: bfloat16 [8, 2000, 32768], P('win', None, 'fibre'), may hold values from -6 to 6
- coupling: float32 [32768], P('fibre'), may hold values from 0.1 to 1
Outputs:
- dispersion: float32 [8192, 400], P('fibre', 'win')
All inputs are finite; a program needn't handle non-finite values.
Results may differ from a plain program's by a relative error of at most 0.0031.
Values may be sent and summed in bfloat16 or wider, within the bound.
No kernel may reach another device: no remote copies, remote signals or barrier semaphores. Data moves between devices by JAX's collectives and lax.ppermute only.
A program may use at most 64 MiB of HBM per device.

v0:
```python
import math

import jax
import jax.numpy as jnp
from jax import lax
from jax.sharding import PartitionSpec as P

SAMPLES = 2000
FREQS = 400
VEL = 512
SEG_BLOCKS = 8


EPS = 1e-06


def from_behind(block, axis, distance):
    devices = range(lax.axis_size(axis))
    route = [(i - distance, i) for i in devices if i - distance in devices]
    return lax.ppermute(block, axis, route)


def from_partner(value, axis, bit):
    mask = 2**bit
    pairs = [(source, source ^ mask) for source in range(lax.axis_size(axis))]
    return lax.ppermute(value, axis, pairs)


def time_table(samples, freqs):
    times = jnp.arange(samples, dtype=jnp.int32)
    bins = jnp.arange(freqs, dtype=jnp.int32) + 1
    phase_int = bins[:, None] * times[None, :] % samples
    angle = 2.0 * math.pi / samples * phase_int.astype(jnp.float32)
    return jnp.concatenate([jnp.cos(angle), jnp.sin(angle)], axis=0).astype(jnp.bfloat16)


def whiten(block, weights, table):
    freqs = table.shape[0] // 2
    raw = jnp.einsum("gt,wtc->wgc", table, block, preferred_element_type=jnp.float32)
    real_part = raw[:, :freqs]
    imag_part = -raw[:, freqs:]
    power = jnp.mean(real_part * real_part + imag_part * imag_part, axis=1, keepdims=True)
    factor = weights[None, None, :] / jnp.sqrt(power + EPS)
    return jnp.concatenate([real_part * factor, imag_part * factor], axis=2).astype(jnp.bfloat16)


def dft_table(inputs, outputs, length):
    rows = jnp.arange(inputs, dtype=jnp.int32)
    cols = jnp.arange(outputs, dtype=jnp.int32)
    angle = 2.0 * math.pi / length * (rows[:, None] * cols[None, :] % length).astype(jnp.float32)
    cosines = jnp.cos(angle)
    sines = jnp.sin(angle)
    upper = jnp.concatenate([cosines, -sines], axis=1)
    lower = jnp.concatenate([sines, cosines], axis=1)
    return jnp.concatenate([upper, lower], axis=0)


def split_table(full_table):
    leading = full_table.astype(jnp.bfloat16)
    trailing = (full_table - leading.astype(jnp.float32)).astype(jnp.bfloat16)
    return (leading, trailing)


def channel_transform(spectra, leading, trailing):
    first = jnp.einsum("wfj,jq->wfq", spectra, leading, preferred_element_type=jnp.float32)
    return first + jnp.einsum("wfj,jq->wfq", spectra, trailing, preferred_element_type=jnp.float32)


def split_product(values, leading, trailing):
    upper_part = values.astype(jnp.bfloat16)
    lower_part = (values - upper_part.astype(jnp.float32)).astype(jnp.bfloat16)
    total = jnp.dot(upper_part, leading, preferred_element_type=jnp.float32)
    total = total + jnp.dot(lower_part, leading, preferred_element_type=jnp.float32)
    return total + jnp.dot(upper_part, trailing, preferred_element_type=jnp.float32)


def phase_image(stack, bin_index, speed_index, width):
    real_part = stack[:, :width]
    imag_part = stack[:, width:]
    power = jnp.mean(real_part * real_part + imag_part * imag_part, axis=1, keepdims=True)
    factor = 1.0 / jnp.sqrt(power + EPS)
    real_part = (real_part * factor).astype(jnp.bfloat16)
    imag_part = (imag_part * factor).astype(jnp.bfloat16)
    lags = jnp.arange(width, dtype=jnp.int32)
    cycles = ((bin_index[:, None] + 1) * lags[None, :]).astype(jnp.float32)
    speed = 150.0 + 1350.0 * speed_index.astype(jnp.float32) / (VEL - 1)
    turns = cycles[:, :, None] * (200.0 * 8.0 / SAMPLES / speed)[None, None, :]
    angle = 2.0 * math.pi * (turns - jnp.floor(turns))
    cosines = jnp.cos(angle).astype(jnp.bfloat16)
    sines = jnp.sin(angle).astype(jnp.bfloat16)
    along = jnp.einsum(
        "fk,fkv->fv", real_part, cosines, preferred_element_type=jnp.float32
    ) + jnp.einsum("fk,fkv->fv", imag_part, sines, preferred_element_type=jnp.float32)
    across = jnp.einsum(
        "fk,fkv->fv", imag_part, cosines, preferred_element_type=jnp.float32
    ) - jnp.einsum("fk,fkv->fv", real_part, sines, preferred_element_type=jnp.float32)
    return ((along * along + across * across) / width).T


def local(samples_data, coupling):
    width = coupling.shape[0]
    table = time_table(samples_data.shape[1], FREQS)
    whitened = whiten(samples_data, coupling, table)
    leading, trailing = split_table(dft_table(width, 2 * width, 2 * width))
    own = channel_transform(whitened, leading, trailing)
    following = from_behind(whitened, "fibre", -1)
    beyond = channel_transform(following, leading, trailing)
    parity = jnp.where(jnp.arange(4 * width, dtype=jnp.int32) % 2 == 0, 1.0, -1.0).astype(
        jnp.float32
    )
    extended = own + parity[None, None, :] * beyond
    own_real = own[..., : 2 * width]
    own_imag = own[..., 2 * width :]
    ext_real = extended[..., : 2 * width]
    ext_imag = extended[..., 2 * width :]
    cross_real = jnp.sum(own_real * ext_real + own_imag * ext_imag, axis=0)
    cross_imag = jnp.sum(own_imag * ext_real - own_real * ext_imag, axis=0)
    inverse_lead, inverse_trail = split_table(dft_table(2 * width, width, 2 * width))
    partial_stack = split_product(
        jnp.concatenate([cross_real, cross_imag], axis=1), inverse_lead, inverse_trail
    ) / (2 * width)
    levels = SEG_BLOCKS.bit_length() - 1
    for level in range(levels):
        partial_stack = partial_stack + from_partner(partial_stack, "fibre", level)
    segment_stack = lax.psum_scatter(partial_stack, "win", scatter_dimension=0, tiled=True)
    bins_here = segment_stack.shape[0]
    speeds_here = VEL // SEG_BLOCKS
    bin_index = lax.axis_index("win") * bins_here + jnp.arange(bins_here, dtype=jnp.int32)
    speed_index = lax.axis_index("fibre") % SEG_BLOCKS * speeds_here + jnp.arange(
        speeds_here, dtype=jnp.int32
    )
    return phase_image(segment_stack, bin_index, speed_index, width)


def solution(mesh):
    placed = (P("win", None, "fibre"), P("fibre"))
    return jax.shard_map(
        local, mesh=mesh, in_specs=placed, out_specs=P("fibre", "win"), check_vma=False
    )
```

profile of v0, /device:TPU:1, one launch (start us, length us, event | category | flops | bytes accessed | tf_op | source)
XLA Modules:
  0.0 282.0 jit_solution(782429188204404022)
XLA Ops:
  6.5 0.0 copy-start
  6.5 0.0 all-reduce.3.cloned.1.call-start
  6.5 14.2 %cosine_convert_fusion.3 = (bf16[400,2000]{1,0:T(8,128)(2,1)S(1)}, bf16[400,2000]{1,0:T(8,128)(2,1)S(1)}) fusion(s32[400]{0:T(512)S(1)} %iota_add_fusion), kind=kLoop, calls=%fused_computation.17 | loop fusion | flops 8800000 | bytes 3201600 | tf_op jit(solution)/shard_map/convert.2
  20.7 0.0 copy-done
  20.7 0.0 copy-start.1
  20.7 1.9 fusion.13
  22.6 0.1 add_reduce_fusion.1
  22.7 0.0 copy-done.1
  22.7 0.1 multiply_convert_fusion.1
  22.9 0.1 pad_maximum_fusion.1
  23.0 1.5 collective-permute-start
  24.5 2.1 fusion.36
  26.5 1.9 fusion.42
  28.5 1.9 fusion.34
  30.4 2.1 fusion.35
  32.5 1.0 fusion.20
  33.5 1.1 convolution_add_fusion
  34.6 4.3 %collective-permute-done = bf16[2,400,512]{2,1,0:T(8,128)(2,1)S(1)} collective-permute-done((bf16[2,400,512]{2,1,0:T(8,128)(2,1)S(1)}, bf16[2,400,512]{2,1,0:T(8,128)(2,1)S(1)}, u32[]{:S(2)}, u32[]{:S(2)}) %collective-permute-start) | collective-permute-done | bytes 819232 | tf_op jit(solution)/shard_map/ppermute | solution.py:20
  38.9 1.0 fusion.68
  39.9 1.0 multiply_add_fusion
  40.9 1.4 add_reduce_fusion
  42.3 0.6 fusion.40
  42.9 0.6 convolution_add_fusion.2
  43.5 0.6 fusion.17
  44.1 9.0 %collective-permute-start.1 = (f32[400,512]{1,0:T(8,128)S(1)}, f32[400,512]{1,0:T(8,128)S(1)}, u32[]{:S(2)}, u32[]{:S(2)}) collective-permute-start(f32[400,512]{1,0:T(8,128)S(1)} %fusion.17), channel_id=1, source_target_pairs={{0,4},{4,0},{8,12},{12,8},{16,20},{20,16},{24,28},{28,24},{32,36},... | collective-permute-start | bytes 2457608 | tf_op jit(solution)/shard_map/ppermute | solution.py:26
  53.1 16.7 %collective-permute-done.1 = f32[400,512]{1,0:T(8,128)S(1)} collective-permute-done((f32[400,512]{1,0:T(8,128)S(1)}, f32[400,512]{1,0:T(8,128)S(1)}, u32[]{:S(2)}, u32[]{:S(2)}) %collective-permute-start.1) | collective-permute-done | bytes 819232 | tf_op jit(solution)/shard_map/ppermute | solution.py:26
  69.9 0.1 add.181
  70.0 6.8 %collective-permute-start.2 = (f32[400,512]{1,0:T(8,128)S(1)}, f32[400,512]{1,0:T(8,128)S(1)}, u32[]{:S(2)}, u32[]{:S(2)}) collective-permute-start(f32[400,512]{1,0:T(8,128)S(1)} %add.181), channel_id=1, source_target_pairs={{0,8},{4,12},{8,0},{12,4},{16,24},{20,28},{24,16},{28,20},{32,40},... | collective-permute-start | bytes 2457608 | tf_op jit(solution)/shard_map/ppermute | solution.py:26
  76.8 16.4 %collective-permute-done.2 = f32[400,512]{1,0:T(8,128)S(1)} collective-permute-done((f32[400,512]{1,0:T(8,128)S(1)}, f32[400,512]{1,0:T(8,128)S(1)}, u32[]{:S(2)}, u32[]{:S(2)}) %collective-permute-start.2) | collective-permute-done | bytes 819232 | tf_op jit(solution)/shard_map/ppermute | solution.py:26
  93.1 0.1 add.182
  93.3 3.5 %collective-permute-start.3 = (f32[400,512]{1,0:T(8,128)S(1)}, f32[400,512]{1,0:T(8,128)S(1)}, u32[]{:S(2)}, u32[]{:S(2)}) collective-permute-start(f32[400,512]{1,0:T(8,128)S(1)} %add.182), channel_id=1, source_target_pairs={{0,16},{4,20},{8,24},{12,28},{16,0},{20,4},{24,8},{28,12},{32,48},... | collective-permute-start | bytes 2457608 | tf_op jit(solution)/shard_map/ppermute | solution.py:26
  96.8 15.6 %collective-permute-done.3 = f32[400,512]{1,0:T(8,128)S(1)} collective-permute-done((f32[400,512]{1,0:T(8,128)S(1)}, f32[400,512]{1,0:T(8,128)S(1)}, u32[]{:S(2)}, u32[]{:S(2)}) %collective-permute-start.3) | collective-permute-done | bytes 819232 | tf_op jit(solution)/shard_map/ppermute | solution.py:26
  112.4 1.1 add.183
  113.4 0.0 all-reduce.3.cloned.1.call-update
  113.5 1.3 dynamic-slice
  115.4 0.1 multiply_convert_fusion.3
  115.5 65.1 %all-reduce.3.cloned.1.call-done = f32[400,512]{1,0:T(8,128)} async-done(((f32[400,512]{1,0:T(8,128)}), f32[400,512]{1,0:T(8,128)}) %all-reduce.3.cloned.1.call-update) | async-done | bytes 819216
  180.6 1.2 add_reduce_fusion.2
  181.8 1.1 fusion.49
  182.9 22.8 %fusion.9 = f32[100,1,64]{2,1,0:T(1,128)S(1)} fusion(f32[64]{0:T(128)S(1)} %add_divide_fusion, f32[100,256]{1,0:T(8,128)S(1)} %multiply_convert_fusion.3, bf16[100,256,1]{1,0,2:T(8,128)(2,1)S(1)} %get-tuple-element.9), kind=kOutput, calls=%fused_computation.14 | convolution fusion | flops 11468800 | bytes 179456 | tf_op jit(solution)/shard_map/fk,fkv->fv/dot_general | solution.py:93
  205.7 22.5 %fusion.6 = f32[100,1,64]{2,1,0:T(1,128)S(1)} fusion(f32[64]{0:T(128)S(1)} %add_divide_fusion, f32[100,256]{1,0:T(8,128)S(1)} %multiply_convert_fusion.3, bf16[100,256,1]{1,0,2:T(8,128)(2,1)S(1)} %get-tuple-element.9), kind=kOutput, calls=%fused_computation.11 | convolution fusion | flops 11468800 | bytes 179456 | tf_op jit(solution)/shard_map/fk,fkv->fv/dot_general | solution.py:94
  228.2 22.5 %fusion.7 = f32[100,1,64]{2,1,0:T(1,128)S(1)} fusion(f32[64]{0:T(128)S(1)} %add_divide_fusion, f32[100,256]{1,0:T(8,128)S(1)} %multiply_convert_fusion.3, bf16[100,256,1]{1,0,2:T(8,128)(2,1)S(1)} %get-tuple-element.10), kind=kOutput, calls=%fused_computation.12 | convolution fusion | flops 11468800 | bytes 179456 | tf_op jit(solution)/shard_map/fk,fkv->fv/dot_general | solution.py:91
  250.7 23.0 %fusion.8 = f32[100,1,64]{2,1,0:T(1,128)S(1)} fusion(f32[64]{0:T(128)S(1)} %add_divide_fusion, f32[100,256]{1,0:T(8,128)S(1)} %multiply_convert_fusion.3, bf16[100,256,1]{1,0,2:T(8,128)(2,1)S(1)} %get-tuple-element.10), kind=kOutput, calls=%fused_computation.13 | convolution fusion | flops 11468800 | bytes 179456 | tf_op jit(solution)/shard_map/fk,fkv->fv/dot_general | solution.py:96
  273.7 0.1 copy.4
  273.8 0.1 copy.6
  273.9 0.1 copy.7
  274.0 0.1 copy.8
  274.1 0.6 fusion.53
  (6 shorter events, 0.0 us)
Async XLA Ops:
  6.5 14.2 %copy-start = (bf16[2,2000,256]{2,1,0:T(8,128)(2,1)S(1)}, bf16[2,2000,256]{2,1,0:T(8,128)(2,1)}, u32[]{:S(2)}) copy-start(bf16[2,2000,256]{2,1,0:T(8,128)(2,1)} %param.2) | copy-start | bytes 6144004
  6.5 174.1 %all-reduce.3.cloned.1.call-start = ((), (), s32[]{:S(2)}) async-start(), calls=%async_computation | async-start | bytes 1638400
  20.7 2.0 copy-start.1
  23.0 15.9 %collective-permute-start = (bf16[2,400,512]{2,1,0:T(8,128)(2,1)S(1)}, bf16[2,400,512]{2,1,0:T(8,128)(2,1)S(1)}, u32[]{:S(2)}, u32[]{:S(2)}) collective-permute-start(bf16[2,400,512]{2,1,0:T(8,128)(2,1)S(1)} %pad_maximum_fusion.1), channel_id=1, source_target_pairs={{4,0},{8,4},{12,8},{16,12},{20,16},{24,20},{28,24},{32,28},{36,32}... | collective-permute-start | bytes 2457608 | tf_op jit(solution)/shard_map/ppermute | solution.py:20
  44.1 25.7 %collective-permute-start.1 = (f32[400,512]{1,0:T(8,128)S(1)}, f32[400,512]{1,0:T(8,128)S(1)}, u32[]{:S(2)}, u32[]{:S(2)}) collective-permute-start(f32[400,512]{1,0:T(8,128)S(1)} %fusion.17), channel_id=1, source_target_pairs={{0,4},{4,0},{8,12},{12,8},{16,20},{20,16},{24,28},{28,24},{32,36},... | collective-permute-start | bytes 2457608 | tf_op jit(solution)/shard_map/ppermute | solution.py:26
  70.0 23.1 %collective-permute-start.2 = (f32[400,512]{1,0:T(8,128)S(1)}, f32[400,512]{1,0:T(8,128)S(1)}, u32[]{:S(2)}, u32[]{:S(2)}) collective-permute-start(f32[400,512]{1,0:T(8,128)S(1)} %add.181), channel_id=1, source_target_pairs={{0,8},{4,12},{8,0},{12,4},{16,24},{20,28},{24,16},{28,20},{32,40},... | collective-permute-start | bytes 2457608 | tf_op jit(solution)/shard_map/ppermute | solution.py:26
  93.3 19.1 %collective-permute-start.3 = (f32[400,512]{1,0:T(8,128)S(1)}, f32[400,512]{1,0:T(8,128)S(1)}, u32[]{:S(2)}, u32[]{:S(2)}) collective-permute-start(f32[400,512]{1,0:T(8,128)S(1)} %add.182), channel_id=1, source_target_pairs={{0,16},{4,20},{8,24},{12,28},{16,0},{20,4},{24,8},{28,12},{32,48},... | collective-permute-start | bytes 2457608 | tf_op jit(solution)/shard_map/ppermute | solution.py:26
Sparse Core Ops, SparseCore 0:
  113.6 66.9 all-reduce.2
where the time goes:
time: 285 us; the launch traced here: 282 us
  waiting for transfers between devices  118 us (41%)
  matrix products  98.6 us (35%)
  other arithmetic  28.2 us (10%)
  starting transfers between devices  20.8 us (7%)
  between operations  14.7 us (5%)
    unnamed x2, waiting for transfers between devices  65.1 us
    ppermute x3, waiting for transfers between devices, from_partner(): return lax.ppermute(value, axis, pairs)  48.6 us
    dot_general x1, matrix products, phase_image(): jnp.einsum('fk,fkv->fv', real_part, sines, preferred_element_type=jnp.flo...  23 us
    dot_general x1, matrix products, phase_image(): jnp.einsum('fk,fkv->fv', imag_part, sines, preferred_element_type=jnp.flo...  22.8 us
    dot_general x1, matrix products, phase_image(): jnp.einsum('fk,fkv->fv', real_part, cosines, preferred_element_type=jnp.f...  22.5 us
    dot_general x1, matrix products, phase_image(): jnp.einsum('fk,fkv->fv', imag_part, cosines, preferred_element_type=jnp.f...  22.5 us
    ppermute x3, starting transfers between devices, from_partner(): return lax.ppermute(value, axis, pairs)  19.3 us
    another operation x2, other arithmetic  14.3 us
  transfers between devices with their start and end apart: 5, of which 5 were waited for; matrix products, arithmetic and copies ran while one was open for 4% of the time, Pallas kernels for 0%

commit v1 on v0

v1 whole, which is shorter than its diff:
```python
import math

import jax
import jax.numpy as jnp
import ml_dtypes
import numpy as np
from jax import lax
from jax.experimental import pallas as pl
from jax.experimental.pallas import tpu as pltpu
from jax.sharding import Mesh, PartitionSpec as P

SAMPLES = 2000
FREQS = 400
OFFS = 256
VEL = 512
SEG_BLOCKS = 8
EPS = 1e-06

WIN_DEVICES = 4
DESTS = SEG_BLOCKS * WIN_DEVICES
CHUNK = FREQS // WIN_DEVICES
TAKEN = -(-CHUNK // SEG_BLOCKS)
SLOT = 16
LOCAL_WINDOWS = 2
DIGIT = 16
BF16 = jnp.bfloat16
F32 = jnp.float32


def bins_of(block, window_device):
    rows = np.arange(SLOT)
    within = TAKEN * block + rows
    valid = (rows < TAKEN) & (within < CHUNK)
    return np.where(valid, window_device * CHUNK + within, -1)


def time_table():
    bins = np.concatenate([bins_of(d // WIN_DEVICES, d % WIN_DEVICES) for d in range(DESTS)])
    times = np.arange(SAMPLES, dtype=np.int64)
    turns = ((bins[:, None] + 1) * times[None, :]) % SAMPLES
    angle = np.float32(2.0 * math.pi / SAMPLES) * turns.astype(np.float32)
    valid = (bins >= 0)[:, None]
    cosines = np.where(valid, np.cos(angle), 0.0).reshape(DESTS, 1, SLOT, SAMPLES)
    sines = np.where(valid, -np.sin(angle), 0.0).reshape(DESTS, 1, SLOT, SAMPLES)
    both = np.concatenate([cosines, sines], axis=1)
    return both.reshape(DESTS * 2 * SLOT, SAMPLES).astype(np.float32).astype(ml_dtypes.bfloat16)


def wave_order():
    return np.concatenate([np.arange(0, 2 * OFFS, 2), np.arange(1, 2 * OFFS, 2)])


def forward_table():
    rows = np.arange(OFFS)
    angle = 2.0 * np.pi / (2 * OFFS) * ((rows[:, None] * wave_order()[None, :]) % (2 * OFFS))
    cosines, sines = np.cos(angle), np.sin(angle)
    upper = np.concatenate([cosines, -sines], axis=1)
    lower = np.concatenate([sines, cosines], axis=1)
    return np.concatenate([upper, lower], axis=0).astype(np.float32).astype(ml_dtypes.bfloat16)


def inverse_tables():
    lags = np.arange(OFFS)
    angle = 2.0 * np.pi / (2 * OFFS) * ((wave_order()[:, None] * lags[None, :]) % (2 * OFFS))
    cosines, sines = np.cos(angle), np.sin(angle)
    upper = np.concatenate([cosines, -sines], axis=1)
    lower = np.concatenate([sines, cosines], axis=1)
    full = (np.concatenate([upper, lower], axis=0) / (2 * OFFS)).astype(np.float32)
    leading = full.astype(ml_dtypes.bfloat16)
    trailing = (full - leading.astype(np.float32)).astype(ml_dtypes.bfloat16)
    return leading, trailing


def spread_table():
    index = np.arange(OFFS)
    same = (index[:, None] % DIGIT) == (index[None, :] % DIGIT)
    return same.astype(ml_dtypes.bfloat16)


def gather_table():
    table = np.zeros((SEG_BLOCKS * SLOT, CHUNK), np.float32)
    for block in range(SEG_BLOCKS):
        for row in range(TAKEN):
            if TAKEN * block + row < CHUNK:
                table[block * SLOT + row, TAKEN * block + row] = 1.0
    return table


def turn_waves(turns):
    rest = turns - jnp.round(turns)
    half = rest * math.pi
    square = half * half
    sine = half * (
        1.0
        + square
        * (
            -1.0 / 6
            + square
            * (1.0 / 120 + square * (-1.0 / 5040 + square * (1.0 / 362880 - square / 39916800)))
        )
    )
    cosine = 1.0 + square * (
        -0.5
        + square
        * (
            1.0 / 24
            + square
            * (
                -1.0 / 720
                + square * (1.0 / 40320 + square * (-1.0 / 3628800 + square / 479001600))
            )
        )
    )
    return 1.0 - 2.0 * sine * sine, 2.0 * sine * cosine


def basis_tables(block, window_device):
    speeds = jnp.arange(VEL, dtype=jnp.int32)
    speed = 150.0 + 1350.0 * speeds.astype(F32) / (VEL - 1)
    slowness = (200.0 * 8.0 / SAMPLES / speed)[None, :]
    first = window_device * CHUNK + TAKEN * block + 1
    index = jnp.arange(SLOT * DIGIT, dtype=jnp.int32)
    fine = ((first + index // DIGIT) * (index % DIGIT)).astype(F32)[:, None]
    coarse = ((first + index % SLOT) * (index // SLOT * DIGIT)).astype(F32)[:, None]
    fine_cos, fine_sin = turn_waves(fine * slowness)
    coarse_cos, coarse_sin = turn_waves(coarse * slowness)
    fine_table = jnp.concatenate([fine_cos, fine_sin], axis=1).astype(BF16)
    coarse_table = jnp.concatenate([coarse_cos, coarse_sin], axis=1)
    return fine_table, coarse_table


WHITEN_STEPS = 8


def whiten_kernel(samples_ref, table_ref, weights_ref, out_ref, raw_ref, power_ref):
    step = pl.program_id(0)
    rows = table_ref.shape[0]
    table = table_ref[...]

    @pl.when(step == 0)
    def _():
        power_ref[...] = jnp.zeros_like(power_ref)

    for w in range(LOCAL_WINDOWS):
        raw = jnp.dot(table, samples_ref[w], preferred_element_type=F32)
        raw_ref[pl.ds(pl.multiple_of(step * rows, rows), rows), w * OFFS : (w + 1) * OFFS] = raw
        power_ref[w] += jnp.sum((raw * raw).reshape(rows // 8, 8, OFFS), axis=0)

    @pl.when(step == WHITEN_STEPS - 1)
    def _():
        for w in range(LOCAL_WINDOWS):
            power = jnp.sum(power_ref[w], axis=0, keepdims=True) / FREQS
            factor = weights_ref[...] / jnp.sqrt(power + EPS)

            def body(d, carry, w=w, factor=factor):
                for part in range(2):
                    start = pl.multiple_of(d * 2 * SLOT + part * SLOT, SLOT)
                    values = raw_ref[pl.ds(start, SLOT), w * OFFS : (w + 1) * OFFS]
                    lane = (2 * w + part) * OFFS
                    out_ref[d, :, lane : lane + OFFS] = (values * factor).astype(BF16)
                return carry

            lax.fori_loop(0, DESTS, body, 0, unroll=4)


def whiten(samples, weights, table):
    rows = table.shape[0] // WHITEN_STEPS
    return pl.pallas_call(
        whiten_kernel,
        grid=(WHITEN_STEPS,),
        in_specs=[
            pl.BlockSpec((LOCAL_WINDOWS, SAMPLES, OFFS), lambda i: (0, 0, 0)),
            pl.BlockSpec((rows, SAMPLES), lambda i: (i, 0)),
            pl.BlockSpec((1, OFFS), lambda i: (0, 0)),
        ],
        out_specs=pl.BlockSpec((DESTS, SLOT, 4 * OFFS), lambda i: (0, 0, 0)),
        out_shape=jax.ShapeDtypeStruct((DESTS, SLOT, 4 * OFFS), BF16),
        scratch_shapes=[
            pltpu.VMEM((table.shape[0], LOCAL_WINDOWS * OFFS), F32),
            pltpu.VMEM((LOCAL_WINDOWS, 8, OFFS), F32),
        ],
        compiler_params=pltpu.CompilerParams(vmem_limit_bytes=40 << 20),
        cost_estimate=pl.CostEstimate(
            flops=2 * table.shape[0] * SAMPLES * 512, bytes_accessed=7 << 20, transcendentals=0
        ),
        name="whiten",
    )(samples, table, weights)


GROUP = WIN_DEVICES * SLOT
WAVES = 2 * OFFS


def own_kernel(recv_ref, table_ref, last_ref, cross_ref, waves_ref):
    table = table_ref[...]
    for w in range(LOCAL_WINDOWS):
        spectra = recv_ref[:, :, w * WAVES : (w + 1) * WAVES].reshape(DESTS * SLOT, WAVES)
        waves_ref[w] = jnp.dot(spectra, table, preferred_element_type=F32)
        last_ref[w] = waves_ref[w, (SEG_BLOCKS - 1) * GROUP : SEG_BLOCKS * GROUP, :]
    for half in range(2):
        real_at = half * OFFS
        imag_at = WAVES + half * OFFS

        def body(step, total, real_at=real_at, imag_at=imag_at, half=half):
            w = step // WIN_DEVICES
            row = pl.multiple_of(step % WIN_DEVICES * SLOT, SLOT)
            total_real, total_imag = total
            own_real = waves_ref[w, pl.ds(row, SLOT), real_at : real_at + OFFS]
            own_imag = waves_ref[w, pl.ds(row, SLOT), imag_at : imag_at + OFFS]
            for block in range(SEG_BLOCKS):
                if block == SEG_BLOCKS - 1:
                    total_real = total_real + (own_real * own_real + own_imag * own_imag)
                    continue
                at = row + (block + 1) * GROUP
                next_real = waves_ref[w, pl.ds(at, SLOT), real_at : real_at + OFFS]
                next_imag = waves_ref[w, pl.ds(at, SLOT), imag_at : imag_at + OFFS]
                if half == 0:
                    ext_real, ext_imag = own_real + next_real, own_imag + next_imag
                else:
                    ext_real, ext_imag = own_real - next_real, own_imag - next_imag
                total_real = total_real + (own_real * ext_real + own_imag * ext_imag)
                total_imag = total_imag + (own_imag * ext_real - own_real * ext_imag)
                own_real, own_imag = next_real, next_imag
            return total_real, total_imag

        zero = jnp.zeros((SLOT, OFFS), F32)
        total = lax.fori_loop(0, LOCAL_WINDOWS * WIN_DEVICES, body, (zero, zero))
        cross_ref[:, real_at : real_at + OFFS] = total[0]
        cross_ref[:, imag_at : imag_at + OFFS] = total[1]


def own_products(received, table):
    return pl.pallas_call(
        own_kernel,
        out_shape=(
            jax.ShapeDtypeStruct((LOCAL_WINDOWS, GROUP, 2 * WAVES), F32),
            jax.ShapeDtypeStruct((SLOT, 2 * WAVES), F32),
        ),
        in_specs=[pl.BlockSpec(memory_space=pltpu.VMEM)] * 2,
        out_specs=(pl.BlockSpec(memory_space=pltpu.VMEM),) * 2,
        scratch_shapes=[pltpu.VMEM((LOCAL_WINDOWS, DESTS * SLOT, 2 * WAVES), F32)],
        compiler_params=pltpu.CompilerParams(vmem_limit_bytes=40 << 20),
        cost_estimate=pl.CostEstimate(
            flops=2 * 1024 * 512 * 1024, bytes_accessed=8 << 20, transcendentals=0
        ),
        name="own_products",
    )(received, table)


def image_kernel(
    halo_ref,
    table_ref,
    last_ref,
    cross_ref,
    lead_ref,
    trail_ref,
    spread_ref,
    fine_ref,
    coarse_ref,
    out_ref,
):
    table = table_ref[...]
    totals = [
        cross_ref[:, at * OFFS : (at + 1) * OFFS] for at in range(4)
    ]
    for w in range(LOCAL_WINDOWS):
        spectra = halo_ref[:, :, w * WAVES : (w + 1) * WAVES].reshape(GROUP, WAVES)
        waves = jnp.dot(spectra, table, preferred_element_type=F32)
        for half in range(2):
            real_at = half * OFFS
            imag_at = WAVES + half * OFFS
            next_real = waves[:, real_at : real_at + OFFS]
            next_imag = waves[:, imag_at : imag_at + OFFS]
            own_real = last_ref[w, :, real_at : real_at + OFFS]
            own_imag = last_ref[w, :, imag_at : imag_at + OFFS]
            more_real = own_real * next_real + own_imag * next_imag
            more_imag = own_imag * next_real - own_real * next_imag
            more_real = jnp.sum(more_real.reshape(WIN_DEVICES, SLOT, OFFS), axis=0)
            more_imag = jnp.sum(more_imag.reshape(WIN_DEVICES, SLOT, OFFS), axis=0)
            sign = 1.0 if half == 0 else -1.0
            totals[half] = totals[half] + sign * more_real
            totals[2 + half] = totals[2 + half] + sign * more_imag
    cross = jnp.concatenate(totals, axis=1)
    upper = cross.astype(BF16)
    lower = (cross - upper.astype(F32)).astype(BF16)
    both = jnp.concatenate([upper, lower], axis=0)
    stack = jnp.dot(both, lead_ref[...], preferred_element_type=F32)
    stack = stack[:SLOT] + stack[SLOT:]
    stack = stack + jnp.dot(upper, trail_ref[...], preferred_element_type=F32)
    real = stack[:, :OFFS]
    imag = stack[:, OFFS:]
    power = jnp.sum(real * real + imag * imag, axis=1, keepdims=True) / OFFS
    factor = 1.0 / jnp.sqrt(power + EPS)
    size = SLOT * DIGIT
    row = lax.broadcasted_iota(jnp.int32, (size, OFFS), 0)
    lane = lax.broadcasted_iota(jnp.int32, (size, OFFS), 1)
    same_digit = row // SLOT == lane // DIGIT
    same_bin = row % SLOT == lane // DIGIT

    def spread(values):
        normed = values * factor
        repeated = jnp.broadcast_to(normed[None], (DIGIT, SLOT, OFFS)).reshape(size, OFFS)
        picked = jnp.where(same_digit, repeated, 0.0).astype(BF16)
        moved = jnp.dot(picked, spread_ref[...], preferred_element_type=F32)
        return jnp.where(same_bin, moved, 0.0).astype(BF16)

    fine = fine_ref[...]
    of_real = jnp.dot(spread(real), fine, preferred_element_type=F32)
    of_imag = jnp.dot(spread(imag), fine, preferred_element_type=F32)
    part_real = of_real[:, :VEL] + of_imag[:, VEL:]
    part_imag = of_imag[:, :VEL] - of_real[:, VEL:]
    coarse_cos = coarse_ref[:, :VEL]
    coarse_sin = coarse_ref[:, VEL:]
    along = part_real * coarse_cos + part_imag * coarse_sin
    across = part_imag * coarse_cos - part_real * coarse_sin
    along = jnp.sum(along.reshape(DIGIT, SLOT, VEL), axis=0)
    across = jnp.sum(across.reshape(DIGIT, SLOT, VEL), axis=0)
    image = (along * along + across * across) / OFFS
    here = VEL // SEG_BLOCKS
    for block in range(SEG_BLOCKS):
        out_ref[block] = image[:, block * here : (block + 1) * here]


def image_of(halo, table, last, cross, lead, trail, spread, fine, coarse):
    return pl.pallas_call(
        image_kernel,
        out_shape=jax.ShapeDtypeStruct((SEG_BLOCKS, SLOT, VEL // SEG_BLOCKS), F32),
        in_specs=[pl.BlockSpec(memory_space=pltpu.VMEM)] * 9,
        out_specs=pl.BlockSpec(memory_space=pltpu.VMEM),
        compiler_params=pltpu.CompilerParams(vmem_limit_bytes=40 << 20),
        cost_estimate=pl.CostEstimate(
            flops=2 * 700 * 512 * 1024, bytes_accessed=6 << 20, transcendentals=0
        ),
        name="image",
    )(halo, table, last, cross, lead, trail, spread, fine, coarse)


def local(samples_data, coupling):
    whitened = whiten(samples_data, coupling[None, :], jnp.asarray(time_table()))
    received = lax.all_to_all(whitened, ("blk", "win"), 0, 0, tiled=True)
    segments = lax.axis_size("seg")
    first_block = received[:WIN_DEVICES]
    halo = lax.ppermute(first_block, "seg", [(s, s - 1) for s in range(1, segments)])
    table = jnp.asarray(forward_table())
    last, cross = own_products(received, table)
    lead, trail = inverse_tables()
    fine, coarse = basis_tables(lax.axis_index("blk"), lax.axis_index("win"))
    parts = image_of(
        halo,
        table,
        last,
        cross,
        jnp.asarray(lead),
        jnp.asarray(trail),
        jnp.asarray(spread_table()),
        fine,
        coarse,
    )
    parts = lax.all_to_all(parts, "blk", 0, 0, tiled=True)
    return lax.dot_general(
        parts.reshape(SEG_BLOCKS * SLOT, VEL // SEG_BLOCKS),
        jnp.asarray(gather_table()),
        (((0,), (0,)), ((), ())),
        precision=lax.Precision.HIGHEST,
        preferred_element_type=F32,
    )


def solution(mesh):
    segments = mesh.shape["fibre"] // SEG_BLOCKS
    inner = Mesh(
        mesh.devices.reshape(segments, SEG_BLOCKS, mesh.shape["win"]), ("seg", "blk", "win")
    )
    placed = (P("win", None, ("seg", "blk")), P(("seg", "blk")))
    return jax.shard_map(
        local, mesh=inner, in_specs=placed, out_specs=P(("seg", "blk"), "win"), check_vma=False
    )
```

time: 285 us -> 66.3 us (0.23)
  the two profiles are of different devices: /device:TPU:1 before, /device:TPU:8 now
where the time goes in v1:
time: 66.3 us; the launch traced here: 65.9 us
  starting transfers between devices  19.8 us (30%)
  waiting for transfers between devices  18.6 us (28%)
  Pallas kernels  9.03 us (14%)
  blocking collectives  8.63 us (13%)
  local copies, waits for them, and re-layouts  5.17 us (8%)
  other arithmetic  3.77 us (6%)
  matrix products  0.88 us (1%)
    all_to_all x1, waiting for transfers between devices, local(): received = lax.all_to_all(whitened, ('blk', 'win'), 0, 0, tiled=True)  15.1 us
    ppermute x1, starting transfers between devices, local(): lax.ppermute(first_block, 'seg', [(s, s - 1) for s in range(1, segments)])  11.9 us
    all_to_all x1, blocking collectives, local(): parts = lax.all_to_all(parts, 'blk', 0, 0, tiled=True)  8.63 us
    all_to_all x1, starting transfers between devices, local(): received = lax.all_to_all(whitened, ('blk', 'win'), 0, 0, tiled=True)  7.91 us
    pallas_call x1, Pallas kernels, whiten(): pl.pallas_call(whiten_kernel, grid=(WHITEN_STEPS,), in_specs=[pl.BlockSpe...  5.11 us
    unnamed x18, local copies, waits for them, and re-layouts  4.65 us
    ppermute x1, waiting for transfers between devices, local(): lax.ppermute(first_block, 'seg', [(s, s - 1) for s in range(1, segments)])  3.46 us
    pallas_call x1, Pallas kernels, own_products(): pl.pallas_call(own_kernel, out_shape=(jax.ShapeDtypeStruct((LOCAL_WINDOWS...  2.1 us
  transfers between devices with their start and end apart: 2, of which 2 were waited for; matrix products, arithmetic and copies ran while one was open for 5% of the time, Pallas kernels for 3%

profile of v1, /device:TPU:8, one launch (start us, length us, event | category | flops | bytes accessed | tf_op | source)
XLA Modules:
  0.0 65.9 jit_solution(10079192850542405536)
XLA Ops:
  0.0 0.0 copy-start.4
  0.0 1.6 %copy-done.4 = bf16[2,2000,256]{2,1,0:T(8,128)(2,1)S(1)} copy-done((bf16[2,2000,256]{2,1,0:T(8,128)(2,1)S(1)}, bf16[2,2000,256]{2,1,0:T(8,128)(2,1)}, u32[]{:S(2)}) %copy-start.4) | copy-done | bytes 2048024
  1.6 0.0 copy-start.5
  1.6 0.7 %copy-done.5 = f32[256]{0:T(256)S(1)} copy-done((f32[256]{0:T(256)S(1)}, f32[256]{0:T(256)}, u32[]{:S(2)}) %copy-start.5) | copy-done | bytes 1048
  2.3 0.0 copy-start.6
  2.3 2.2 %copy-done.6 = bf16[1024,2000]{1,0:T(8,128)(2,1)S(1)} copy-done((bf16[1024,2000]{1,0:T(8,128)(2,1)S(1)}, bf16[1024,2000]{1,0:T(8,128)(2,1)}, u32[]{:S(2)}) %copy-start.6) | copy-done | bytes 4096024
  4.4 5.1 %whiten.1 = bf16[32,16,1024]{2,1,0:T(8,128)(2,1)} custom-call(bf16[2,2000,256]{2,1,0:T(8,128)(2,1)S(1)} %copy-done.4, bf16[1024,2000]{1,0:T(8,128)(2,1)S(1)} %copy-done.6, f32[1,256]{1,0:T(1,128)S(1)} %bitcast.4), custom_call_target="tpu_custom_call" | custom-call | flops 2097152000 | bytes 7340032 | tf_op jit(solution)/shard_map/whiten/pallas_call | solution.py:168
  9.6 0.0 copy-start
  9.6 7.9 %all-to-all-start = ((bf16[32,16,1024]{2,1,0:T(8,128)(2,1)}), bf16[32,16,1024]{2,1,0:T(8,128)(2,1)S(1)}, u32[]{:S(2)}, u32[]{:S(2)}) async-start(bf16[32,16,1024]{2,1,0:T(8,128)(2,1)} %whiten.1), calls=%async_computation | async-start | bytes 2097152 | tf_op jit(solution)/shard_map/all_to_all | solution.py:340
  17.5 0.0 copy-start.3
  17.5 1.9 %fusion.3 = (f32[256,512]{1,0:T(8,128)S(1)}, f32[256,512]{1,0:T(8,128)S(1)}, bf16[256,512]{1,0:T(8,128)(2,1)S(1)}, bf16[256,512]{1,0:T(8,128)(2,1)}) fusion(f32[512]{0:T(512)S(1)} %add_divide_fusion, f32[256]{0:T(256)S(1)} %get-tuple-element.15, f32[256]{0:T(256)S(1)} %get-tuple-element.16), kind=kLoop, calls=%fused_computation.10 | loop fusion | flops 8650752 | bytes 1576960 | tf_op jit(solution)/shard_map/sub | solution.py:114
  19.5 0.1 pad_maximum_fusion.coarse_ref
  19.6 15.1 %all-to-all-done.recv_ref = bf16[32,16,1024]{2,1,0:T(8,128)(2,1)S(1)} async-done(((bf16[32,16,1024]{2,1,0:T(8,128)(2,1)}), bf16[32,16,1024]{2,1,0:T(8,128)(2,1)S(1)}, u32[]{:S(2)}, u32[]{:S(2)}) %all-to-all-start) | async-done | bytes 1048608 | tf_op jit(solution)/shard_map/all_to_all | solution.py:340
  34.6 0.0 copy-start.1
  34.6 0.0 copy-start.2
  34.7 11.9 %collective-permute-start = (bf16[4,16,1024]{2,1,0:T(8,128)(2,1)S(1)}, bf16[4,16,1024]{2,1,0:T(8,128)(2,1)S(1)}, u32[]{:S(2)}, u32[]{:S(2)}) collective-permute-start(bf16[4,16,1024]{2,1,0:T(8,128)(2,1)S(1)} %slice.4), channel_id=1, source_target_pairs={{32,0},{64,32},{96,64},{128,96},{160,128},{192,160},{224,192},{256... | collective-permute-start | bytes 393224 | tf_op jit(solution)/shard_map/ppermute | solution.py:343
  46.5 1.0 %pad_maximum_fusion.1.fine_ref = bf16[256,1024]{1,0:T(8,128)(2,1)S(1)} fusion(bf16[256,512]{1,0:T(8,128)(2,1)S(1)} %get-tuple-element.13, bf16[256,512]{1,0:T(8,128)(2,1)} %get-tuple-element.14), kind=kLoop, calls=%fused_computation.13 | loop fusion | flops 1048576 | bytes 1048576 | tf_op jit(solution)/shard_map/concatenate | solution.py:127
  47.6 0.0 copy-done
  47.6 0.0 copy-start.7
  47.6 2.1 %own_products.1 = (f32[2,64,1024]{2,1,0:T(8,128)S(1)}, f32[16,1024]{1,0:T(8,128)S(1)}) custom-call(bf16[32,16,1024]{2,1,0:T(8,128)(2,1)S(1)} %all-to-all-done.recv_ref, bf16[512,1024]{1,0:T(8,128)(2,1)S(1)} %copy-done), custom_call_target="tpu_custom_call" | custom-call | flops 1073741824 | bytes 8388608 | tf_op jit(solution)/shard_map/own_products/pallas_call | solution.py:233
  49.7 3.5 %collective-permute-done.halo_ref = bf16[4,16,1024]{2,1,0:T(8,128)(2,1)S(1)} collective-permute-done((bf16[4,16,1024]{2,1,0:T(8,128)(2,1)S(1)}, bf16[4,16,1024]{2,1,0:T(8,128)(2,1)S(1)}, u32[]{:S(2)}, u32[]{:S(2)}) %collective-permute-start) | collective-permute-done | bytes 131104 | tf_op jit(solution)/shard_map/ppermute | solution.py:343
  53.2 0.0 copy-done.3
  53.2 0.0 copy-done.1
  53.2 0.0 copy-done.2
  53.2 1.8 %image.1 = f32[8,16,64]{2,1,0:T(8,128)S(1)} custom-call(bf16[4,16,1024]{2,1,0:T(8,128)(2,1)S(1)} %collective-permute-done.halo_ref, bf16[512,1024]{1,0:T(8,128)(2,1)S(1)} %copy-done, f32[2,64,1024]{2,1,0:T(8,128)S(1)} %get-tuple-element.7.last_ref, f32[16,1024]{1,0:T(8,128)S(1)} %get-tuple-element.8.cross_ref, bf16[1024,512]{1,0:T(8,128)(2,1)S(1)} %copy-done.1, ...), custom_call_target="tpu_custom_call" | custom-call | flops 734003200 | bytes 6291456 | tf_op jit(solution)/shard_map/image/pallas_call | solution.py:325
  55.0 0.1 reshape.40
  55.1 8.6 %all_to_all.10 = f32[8,1,1024]{2,1,0:T(1,128)S(1)} all-to-all(f32[8,1,1024]{2,1,0:T(1,128)S(1)} %reshape.40), channel_id=1, replica_groups=mesh['seg'=16,'blk'=8,'win'=4] {'blk'}, dimensions={0} | all-to-all | bytes 65536 | tf_op jit(solution)/shard_map/all_to_all | solution.py:359
  63.7 0.5 broadcast.269
  64.2 0.7 %reduce = f32[8,1024]{1,0:T(8,128)S(1)} reduce(f32[8,1,1024]{2,1,0:T(1,128)S(1)} %all_to_all.10, f32[]{:T(128)} %broadcast.269), dimensions={1}, to_apply=%all_to_all.7.reduce_sub_computation | reduce | bytes 65540 | tf_op jit(solution)/shard_map/all_to_all | solution.py:359
  65.0 0.1 reshape.41
  65.0 0.0 copy-done.7
  65.0 0.9 %fusion.14 = f32[64,100]{1,0:T(8,128)} fusion(f32[128,64]{1,0:T(8,128)S(1)} %bitcast.5, f32[128,100]{1,0:T(8,128)S(1)} %copy-done.7), kind=kOutput, calls=%fused_computation.38 | convolution fusion | flops 9830400 | bytes 109568 | tf_op jit(solution)/shard_map/dot_general | solution.py:360
  (3 shorter events, 0.0 us)
Async XLA Ops:
  0.0 1.6 %copy-start.4 = (bf16[2,2000,256]{2,1,0:T(8,128)(2,1)S(1)}, bf16[2,2000,256]{2,1,0:T(8,128)(2,1)}, u32[]{:S(2)}) copy-start(bf16[2,2000,256]{2,1,0:T(8,128)(2,1)} %samples_ref.1) | copy-start | bytes 6144004
  1.6 0.7 %copy-start.5 = (f32[256]{0:T(256)S(1)}, f32[256]{0:T(256)}, u32[]{:S(2)}) copy-start(f32[256]{0:T(256)} %param.9) | copy-start | bytes 3076
  2.3 2.2 %copy-start.6 = (bf16[1024,2000]{1,0:T(8,128)(2,1)S(1)}, bf16[1024,2000]{1,0:T(8,128)(2,1)}, u32[]{:S(2)}) copy-start(bf16[1024,2000]{1,0:T(8,128)(2,1)} %constant.106.clone.table_ref) | copy-start | bytes 12288004
  9.6 38.0 %copy-start = (bf16[512,1024]{1,0:T(8,128)(2,1)S(1)}, bf16[512,1024]{1,0:T(8,128)(2,1)}, u32[]{:S(2)}) copy-start(bf16[512,1024]{1,0:T(8,128)(2,1)} %constant.107.clone.table_ref) | copy-start | bytes 3145732
  9.6 25.1 %all-to-all-start = ((bf16[32,16,1024]{2,1,0:T(8,128)(2,1)}), bf16[32,16,1024]{2,1,0:T(8,128)(2,1)S(1)}, u32[]{:S(2)}, u32[]{:S(2)}) async-start(bf16[32,16,1024]{2,1,0:T(8,128)(2,1)} %whiten.1), calls=%async_computation | async-start | bytes 2097152 | tf_op jit(solution)/shard_map/all_to_all | solution.py:340
  17.5 35.6 %copy-start.3 = (bf16[256,256]{1,0:T(8,128)(2,1)S(1)}, bf16[256,256]{1,0:T(8,128)(2,1)}, u32[]{:S(2)}) copy-start(bf16[256,256]{1,0:T(8,128)(2,1)} %constant.110.clone.spread_ref) | copy-start | bytes 393220
  34.6 18.5 %copy-start.1 = (bf16[1024,512]{1,0:T(8,128)(2,1)S(1)}, bf16[1024,512]{1,0:T(8,128)(2,1)}, u32[]{:S(2)}) copy-start(bf16[1024,512]{1,0:T(8,128)(2,1)} %constant.108.clone.lead_ref) | copy-start | bytes 3145732
  34.6 18.5 %copy-start.2 = (bf16[1024,512]{1,0:T(8,128)(2,1)S(1)}, bf16[1024,512]{1,0:T(8,128)(2,1)}, u32[]{:S(2)}) copy-start(bf16[1024,512]{1,0:T(8,128)(2,1)} %constant.109.clone.trail_ref) | copy-start | bytes 3145732
  34.7 18.5 %collective-permute-start = (bf16[4,16,1024]{2,1,0:T(8,128)(2,1)S(1)}, bf16[4,16,1024]{2,1,0:T(8,128)(2,1)S(1)}, u32[]{:S(2)}, u32[]{:S(2)}) collective-permute-start(bf16[4,16,1024]{2,1,0:T(8,128)(2,1)S(1)} %slice.4), channel_id=1, source_target_pairs={{32,0},{64,32},{96,64},{128,96},{160,128},{192,160},{224,192},{256... | collective-permute-start | bytes 393224 | tf_op jit(solution)/shard_map/ppermute | solution.py:343
  47.6 17.5 %copy-start.7 = (f32[128,100]{1,0:T(8,128)S(1)}, f32[128,100]{1,0:T(8,128)}, u32[]{:S(2)}) copy-start(f32[128,100]{1,0:T(8,128)} %constant.111.clone) | copy-start | bytes 153604

commit v2 on v1

v2 whole, which is shorter than its diff:
```python
import math

import jax
import jax.numpy as jnp
import ml_dtypes
import numpy as np
from jax import lax
from jax.experimental import pallas as pl
from jax.experimental.pallas import tpu as pltpu
from jax.sharding import Mesh, PartitionSpec as P

SAMPLES = 2000
FREQS = 400
OFFS = 256
VEL = 512
SEG_BLOCKS = 8
EPS = 1e-06

WIN_DEVICES = 4
DESTS = SEG_BLOCKS * WIN_DEVICES
CHUNK = FREQS // WIN_DEVICES
FIRST_BIN = [0, 12, 26, 38, 50, 62, 76, 88, CHUNK]
SLOT = 16
TILE = 8
SENT = 7 * TILE
TAKEN = 4 * TILE
LOCAL_WINDOWS = 2
DIGIT = 16
ROWS = DESTS // 2 * SENT
STEP = 256
STEPS = 4
HALF = SAMPLES // 2
LANES = 128
BF16 = jnp.bfloat16
F32 = jnp.float32


def bins_of(block, window_device):
    rows = np.arange(SLOT)
    within = FIRST_BIN[block] + rows
    return np.where(within < FIRST_BIN[block + 1], window_device * CHUNK + within, -1)


def table_rows():
    bins, parts = [], []
    for pair in range(DESTS // 2):
        dests = [bins_of(d // WIN_DEVICES, d % WIN_DEVICES) for d in (2 * pair, 2 * pair + 1)]
        own = []
        for dest in dests:
            own.append(
                [(dest[r], 0) for r in range(8)]
                + [(dest[r], 1) for r in range(8)]
                + [(dest[r], 0) for r in range(8, 12)]
                + [(dest[r], 1) for r in range(8, 12)]
            )
        mixed = [(dest[r], part) for part in (0, 1) for dest in dests for r in (12, 13)]
        for at, part in own[0] + mixed + own[1]:
            bins.append(at)
            parts.append(part)
    return np.array(bins), np.array(parts)


def time_table():
    bins, parts = table_rows()
    times = np.arange(STEP * STEPS, dtype=np.int64)
    turns = ((bins[:, None] + 1) * times[None, :]) % SAMPLES
    angle = np.float32(2.0 * math.pi / SAMPLES) * turns.astype(np.float32)
    valid = (bins >= 0)[:, None] & (times < SAMPLES // 2)[None, :]
    waves = np.where(parts[:, None] == 0, np.cos(angle), -np.sin(angle))
    table = np.where(valid, waves, 0.0).reshape(ROWS, STEPS, STEP)
    return table.transpose(1, 0, 2).astype(np.float32).astype(ml_dtypes.bfloat16)


def wave_order():
    return np.concatenate([np.arange(0, 2 * OFFS, 2), np.arange(1, 2 * OFFS, 2)])


def forward_table():
    rows = np.arange(OFFS)
    angle = 2.0 * np.pi / (2 * OFFS) * ((rows[:, None] * wave_order()[None, :]) % (2 * OFFS))
    cosines, sines = np.cos(angle), np.sin(angle)
    upper = np.concatenate([cosines, -sines], axis=1)
    lower = np.concatenate([sines, cosines], axis=1)
    return np.concatenate([upper, lower], axis=0).astype(np.float32).astype(ml_dtypes.bfloat16)


def inverse_table():
    lags = np.arange(OFFS)
    angle = 2.0 * np.pi / (2 * OFFS) * ((wave_order()[:, None] * lags[None, :]) % (2 * OFFS))
    cosines, sines = np.cos(angle), np.sin(angle)
    upper = np.concatenate([cosines, -sines], axis=1)
    lower = np.concatenate([sines, cosines], axis=1)
    full = (np.concatenate([upper, lower], axis=0) / (2 * OFFS)).astype(np.float32)
    return full.astype(ml_dtypes.bfloat16)


def spread_table():
    index = np.arange(OFFS)
    same = (index[:, None] % DIGIT) == (index[None, :] % DIGIT)
    return same.astype(ml_dtypes.bfloat16)


def gather_table():
    table = np.zeros((SEG_BLOCKS * SLOT, CHUNK), np.float32)
    for block in range(SEG_BLOCKS):
        for row in range(FIRST_BIN[block + 1] - FIRST_BIN[block]):
            table[block * SLOT + row, FIRST_BIN[block] + row] = 1.0
    return table


def turn_waves(turns):
    rest = turns - jnp.round(turns)
    half = rest * math.pi
    square = half * half
    sine = half * (
        1.0
        + square
        * (
            -1.0 / 6
            + square
            * (1.0 / 120 + square * (-1.0 / 5040 + square * (1.0 / 362880 - square / 39916800)))
        )
    )
    cosine = 1.0 + square * (
        -0.5
        + square
        * (
            1.0 / 24
            + square
            * (
                -1.0 / 720
                + square * (1.0 / 40320 + square * (-1.0 / 3628800 + square / 479001600))
            )
        )
    )
    return 1.0 - 2.0 * sine * sine, 2.0 * sine * cosine


def basis_tables(block, window_device):
    speeds = jnp.arange(VEL, dtype=jnp.int32)
    speed = 150.0 + 1350.0 * speeds.astype(F32) / (VEL - 1)
    slowness = (200.0 * 8.0 / SAMPLES / speed)[None, :]
    first = window_device * CHUNK + (25 * block + 2) // 4 * 2 + 1
    index = jnp.arange(SLOT * DIGIT, dtype=jnp.int32)
    fine = ((first + index // DIGIT) * (index % DIGIT)).astype(F32)[:, None]
    coarse = ((first + index % SLOT) * (index // SLOT * DIGIT)).astype(F32)[:, None]
    fine_cos, fine_sin = turn_waves(fine * slowness)
    coarse_cos, coarse_sin = turn_waves(coarse * slowness)
    fine_table = jnp.concatenate([fine_cos, fine_sin], axis=1).astype(BF16)
    coarse_table = jnp.concatenate([coarse_cos, coarse_sin], axis=1)
    return fine_table, coarse_table


def whiten_kernel(
    samples_hbm,
    table_hbm,
    weights_hbm,
    out_hbm,
    early_ref,
    late_ref,
    table_ref,
    weights_ref,
    raw_ref,
    out_ref,
    in_sems,
    out_sems,
):
    weights_copy = pltpu.make_async_copy(weights_hbm, weights_ref, in_sems.at[3 * STEPS])
    copies = []
    for step in range(STEPS):
        early = STEP
        late_at = 992 + step * STEP
        late = min(STEP + 16, SAMPLES - late_at)
        copies.append(
            [
                pltpu.make_async_copy(
                    table_hbm.at[step], table_ref.at[step], in_sems.at[3 * step]
                ),
                pltpu.make_async_copy(
                    samples_hbm.at[:, pl.ds(step * STEP, early), :],
                    early_ref.at[step, :, pl.ds(0, early), :],
                    in_sems.at[3 * step + 1],
                ),
                pltpu.make_async_copy(
                    samples_hbm.at[:, pl.ds(late_at, late), :],
                    late_ref.at[step, :, pl.ds(0, late), :],
                    in_sems.at[3 * step + 2],
                ),
            ]
        )
        for copy in copies[-1]:
            copy.start()
    weights_copy.start()

    row = lax.broadcasted_iota(jnp.int32, (SLOT, STEP), 0)
    sign = jnp.where(row % 2 == 0, -1.0, 1.0).astype(BF16)
    tile_row = lax.broadcasted_iota(jnp.int32, (TILE, OFFS), 0)
    upper_half = tile_row < 4
    upper_pair = tile_row % 4 < 2
    missing = HALF - (STEPS - 1) * STEP + 8
    late_ref[STEPS - 1, :, missing:, :] = jnp.zeros(
        (LOCAL_WINDOWS, STEP + 16 - missing, OFFS), BF16
    )
    powers = None
    for step in range(STEPS):
        for copy in copies[step]:
            copy.wait()
        table = table_ref[step]
        turned = (table.reshape(ROWS // SLOT, SLOT, STEP) * sign[None]).reshape(ROWS, STEP)
        pair = jnp.concatenate([table, turned], axis=1)
        samples = jnp.concatenate(
            [
                jnp.concatenate(
                    [early_ref[step, w], late_ref[step, w, 8 : 8 + STEP, :]], axis=0
                )
                for w in range(LOCAL_WINDOWS)
            ],
            axis=1,
        )
        raw = jnp.dot(pair, samples, preferred_element_type=F32)
        if step > 0:
            raw = raw + raw_ref[...]
        raw_ref[...] = raw
        if step == STEPS - 1:
            powers = jnp.sum((raw * raw).reshape(ROWS // 8, 8, LOCAL_WINDOWS * OFFS), axis=0)

    weights_copy.wait()
    factors = []
    for w in range(LOCAL_WINDOWS):
        power = jnp.sum(powers[:, w * OFFS : (w + 1) * OFFS], axis=0, keepdims=True) / FREQS
        factors.append(weights_ref[...] / jnp.sqrt(power + EPS))
    done = []
    for part in range(OUT_PARTS):
        first = part * (DESTS // OUT_PARTS)
        for pair in range(first // 2, (first + DESTS // OUT_PARTS) // 2):
            values = [
                raw_ref[pair * SENT : (pair + 1) * SENT, w * OFFS : (w + 1) * OFFS] * factors[w]
                for w in range(LOCAL_WINDOWS)
            ]
            mixed = [value[3 * TILE : 4 * TILE] for value in values]
            for odd in range(2):
                one, two = [value[4 * odd * TILE : (4 * odd + 3) * TILE] for value in values]
                ends = [one[2 * TILE :], two[2 * TILE :]]
                pieces = [
                    one[: 2 * TILE],
                    two[: 2 * TILE],
                    jnp.where(upper_half, ends[0], pltpu.roll(ends[1], 4, 0)),
                    jnp.where(upper_half, pltpu.roll(ends[0], 4, 0), ends[1]),
                ]
                if odd == 0:
                    pieces.append(jnp.where(upper_pair, mixed[0], pltpu.roll(mixed[1], 2, 0)))
                else:
                    pieces.append(jnp.where(upper_pair, pltpu.roll(mixed[0], 6, 0), mixed[1]))
                out_ref[2 * pair + odd] = jnp.concatenate(pieces, axis=0).astype(BF16)
        here = pl.ds(first, DESTS // OUT_PARTS)
        done.append(pltpu.make_async_copy(out_ref.at[here], out_hbm.at[here], out_sems.at[part]))
        done[-1].start()
    for copy in done:
        copy.wait()


OUT_PARTS = 4


def whiten(samples, weights, table):
    return pl.pallas_call(
        whiten_kernel,
        in_specs=[pl.BlockSpec(memory_space=pl.ANY)] * 3,
        out_specs=pl.BlockSpec(memory_space=pl.ANY),
        out_shape=jax.ShapeDtypeStruct((DESTS, SENT, OFFS), BF16),
        scratch_shapes=[
            pltpu.VMEM((STEPS, LOCAL_WINDOWS, STEP, OFFS), BF16),
            pltpu.VMEM((STEPS, LOCAL_WINDOWS, STEP + 16, OFFS), BF16),
            pltpu.VMEM((STEPS, ROWS, STEP), BF16),
            pltpu.VMEM((1, OFFS), F32),
            pltpu.VMEM((ROWS, LOCAL_WINDOWS * OFFS), F32),
            pltpu.VMEM((DESTS, SENT, OFFS), BF16),
            pltpu.SemaphoreType.DMA((3 * STEPS + 1,)),
            pltpu.SemaphoreType.DMA((OUT_PARTS,)),
        ],
        compiler_params=pltpu.CompilerParams(vmem_limit_bytes=62 << 20),
        cost_estimate=pl.CostEstimate(
            flops=2 * ROWS * SAMPLES * 512, bytes_accessed=5 << 20, transcendentals=0
        ),
        name="whiten",
    )(samples, table, weights)


GROUP = WIN_DEVICES * TAKEN
WAVES = 2 * OFFS


def side_by_side(slot):
    values = slot.astype(F32)
    tiles = [values[at * TILE : (at + 1) * TILE] for at in range(7)]
    real = jnp.concatenate([tiles[0], tiles[2], tiles[4], tiles[6]], axis=0)
    imag = jnp.concatenate(
        [tiles[1], tiles[3], tiles[5], pltpu.roll(tiles[6], 4, 0)], axis=0
    )
    return jnp.concatenate([real, imag], axis=1).astype(BF16)


def by_bin(values):
    tile_row = lax.broadcasted_iota(jnp.int32, (TILE, values.shape[1]), 0)
    tiles = [values[at * TILE : (at + 1) * TILE] for at in range(4)]
    four = tiles[2] + pltpu.roll(tiles[2], 4, 0)
    two = pltpu.roll(tiles[3] + pltpu.roll(tiles[3], 6, 0), 4, 0)
    rest = jnp.where(tile_row < 4, four, jnp.where(tile_row < 6, two, 0.0))
    return jnp.concatenate([tiles[0] + tiles[1], rest], axis=0)


def own_kernel(recv_ref, table_ref, last_ref, cross_ref, slots_ref, waves_ref):
    for source in range(DESTS):
        slots_ref[source * TAKEN : (source + 1) * TAKEN] = side_by_side(recv_ref[source])
    waves_ref[...] = jnp.dot(slots_ref[...], table_ref[...], preferred_element_type=F32)
    last_ref[...] = waves_ref[(SEG_BLOCKS - 1) * GROUP :, :]
    for half in range(2):
        real_at = half * OFFS
        imag_at = WAVES + half * OFFS

        def body(step, total, real_at=real_at, imag_at=imag_at, half=half):
            row = pl.multiple_of(step * TAKEN, TAKEN)
            total_real, total_imag = total
            own_real = waves_ref[pl.ds(row, TAKEN), real_at : real_at + OFFS]
            own_imag = waves_ref[pl.ds(row, TAKEN), imag_at : imag_at + OFFS]
            for block in range(SEG_BLOCKS):
                if block == SEG_BLOCKS - 1:
                    total_real = total_real + (own_real * own_real + own_imag * own_imag)
                    continue
                at = row + (block + 1) * GROUP
                next_real = waves_ref[pl.ds(at, TAKEN), real_at : real_at + OFFS]
                next_imag = waves_ref[pl.ds(at, TAKEN), imag_at : imag_at + OFFS]
                if half == 0:
                    ext_real, ext_imag = own_real + next_real, own_imag + next_imag
                else:
                    ext_real, ext_imag = own_real - next_real, own_imag - next_imag
                total_real = total_real + (own_real * ext_real + own_imag * ext_imag)
                total_imag = total_imag + (own_imag * ext_real - own_real * ext_imag)
                own_real, own_imag = next_real, next_imag
            return total_real, total_imag

        zero = jnp.zeros((TAKEN, OFFS), F32)
        total = lax.fori_loop(0, WIN_DEVICES, body, (zero, zero))
        cross_ref[:, real_at : real_at + OFFS] = total[0]
        cross_ref[:, imag_at : imag_at + OFFS] = total[1]


def own_products(received, table):
    return pl.pallas_call(
        own_kernel,
        out_shape=(
            jax.ShapeDtypeStruct((GROUP, 2 * WAVES), F32),
            jax.ShapeDtypeStruct((TAKEN, 2 * WAVES), F32),
        ),
        in_specs=[pl.BlockSpec(memory_space=pltpu.VMEM)] * 2,
        out_specs=(pl.BlockSpec(memory_space=pltpu.VMEM),) * 2,
        scratch_shapes=[
            pltpu.VMEM((DESTS * TAKEN, WAVES), BF16),
            pltpu.VMEM((DESTS * TAKEN, 2 * WAVES), F32),
        ],
        compiler_params=pltpu.CompilerParams(vmem_limit_bytes=40 << 20),
        cost_estimate=pl.CostEstimate(
            flops=2 * 1024 * 512 * 1024, bytes_accessed=8 << 20, transcendentals=0
        ),
        name="own_products",
    )(received, table)


def image_kernel(
    halo_ref,
    table_ref,
    last_ref,
    cross_ref,
    lead_ref,
    spread_ref,
    fine_ref,
    coarse_ref,
    out_ref,
):
    totals = [
        cross_ref[:, at * OFFS : (at + 1) * OFFS] for at in range(4)
    ]
    spectra = jnp.concatenate([side_by_side(halo_ref[w]) for w in range(WIN_DEVICES)], axis=0)
    waves = jnp.dot(spectra, table_ref[...], preferred_element_type=F32)
    for half in range(2):
        real_at = half * OFFS
        imag_at = WAVES + half * OFFS
        next_real = waves[:, real_at : real_at + OFFS]
        next_imag = waves[:, imag_at : imag_at + OFFS]
        own_real = last_ref[:, real_at : real_at + OFFS]
        own_imag = last_ref[:, imag_at : imag_at + OFFS]
        more_real = own_real * next_real + own_imag * next_imag
        more_imag = own_imag * next_real - own_real * next_imag
        more_real = jnp.sum(more_real.reshape(WIN_DEVICES, TAKEN, OFFS), axis=0)
        more_imag = jnp.sum(more_imag.reshape(WIN_DEVICES, TAKEN, OFFS), axis=0)
        sign = 1.0 if half == 0 else -1.0
        totals[half] = totals[half] + sign * more_real
        totals[2 + half] = totals[2 + half] + sign * more_imag
    cross = by_bin(jnp.concatenate(totals, axis=1))
    flat_real = jnp.sum(cross[:, :WAVES], axis=1, keepdims=True) / WAVES
    flat_imag = jnp.sum(cross[:, WAVES:], axis=1, keepdims=True) / WAVES
    cross = jnp.concatenate([cross[:, :WAVES] - flat_real, cross[:, WAVES:] - flat_imag], axis=1)
    upper = cross.astype(BF16)
    lower = (cross - upper.astype(F32)).astype(BF16)
    both = jnp.concatenate([upper, lower], axis=0)
    stack = jnp.dot(both, lead_ref[...], preferred_element_type=F32)
    stack = stack[:SLOT] + stack[SLOT:]
    lag = lax.broadcasted_iota(jnp.int32, (SLOT, 2 * OFFS), 1)
    stack = stack + jnp.where(lag == 0, flat_real, jnp.where(lag == OFFS, flat_imag, 0.0))
    real = stack[:, :OFFS]
    imag = stack[:, OFFS:]
    power = jnp.sum(real * real + imag * imag, axis=1, keepdims=True) / OFFS
    factor = 1.0 / jnp.sqrt(power + EPS)
    size = SLOT * DIGIT
    row = lax.broadcasted_iota(jnp.int32, (size, OFFS), 0)
    lane = lax.broadcasted_iota(jnp.int32, (size, OFFS), 1)
    same_digit = row // SLOT == lane // DIGIT
    same_bin = row % SLOT == lane // DIGIT

    def spread(values):
        normed = values * factor
        repeated = jnp.broadcast_to(normed[None], (DIGIT, SLOT, OFFS)).reshape(size, OFFS)
        picked = jnp.where(same_digit, repeated, 0.0).astype(BF16)
        moved = jnp.dot(picked, spread_ref[...], preferred_element_type=F32)
        return jnp.where(same_bin, moved, 0.0).astype(BF16)

    of_both = jnp.dot(
        jnp.concatenate([spread(real), spread(imag)], axis=0),
        fine_ref[...],
        preferred_element_type=F32,
    )
    part_real = of_both[:size, :VEL] + of_both[size:, VEL:]
    part_imag = of_both[size:, :VEL] - of_both[:size, VEL:]
    coarse_cos = coarse_ref[:, :VEL]
    coarse_sin = coarse_ref[:, VEL:]
    along = part_real * coarse_cos + part_imag * coarse_sin
    across = part_imag * coarse_cos - part_real * coarse_sin
    along = jnp.sum(along.reshape(DIGIT, SLOT, VEL), axis=0)
    across = jnp.sum(across.reshape(DIGIT, SLOT, VEL), axis=0)
    image = (along * along + across * across) / OFFS
    here = VEL // SEG_BLOCKS
    for block in range(SEG_BLOCKS):
        pair = image[:, block // 2 * LANES : (block // 2 + 1) * LANES]
        out_ref[block] = pair if block % 2 == 0 else jnp.roll(pair, here, axis=1)


def image_of(halo, table, last, cross, lead, spread, fine, coarse):
    return pl.pallas_call(
        image_kernel,
        out_shape=jax.ShapeDtypeStruct((SEG_BLOCKS, SLOT, LANES), F32),
        in_specs=[pl.BlockSpec(memory_space=pltpu.VMEM)] * 8,
        out_specs=pl.BlockSpec(memory_space=pltpu.VMEM),
        compiler_params=pltpu.CompilerParams(vmem_limit_bytes=40 << 20),
        cost_estimate=pl.CostEstimate(
            flops=2 * 700 * 512 * 1024, bytes_accessed=6 << 20, transcendentals=0
        ),
        name="image",
    )(halo, table, last, cross, lead, spread, fine, coarse)


def gather(parts, table):
    rows = parts.reshape(SEG_BLOCKS * SLOT, LANES)
    gathered = lax.dot_general(
        rows,
        table,
        (((0,), (0,)), ((), ())),
        precision=lax.Precision.HIGHEST,
        preferred_element_type=F32,
    )
    return gathered[: VEL // SEG_BLOCKS]


def local(samples_data, coupling):
    whitened = whiten(samples_data, coupling[None, :], jnp.asarray(time_table()))
    received = lax.all_to_all(whitened, ("blk", "win"), 0, 0, tiled=True)
    segments = lax.axis_size("seg")
    first_block = received[:WIN_DEVICES]
    halo = lax.ppermute(first_block, "seg", [(s, s - 1) for s in range(1, segments)])
    table = jnp.asarray(forward_table())
    last, cross = own_products(received, table)
    fine, coarse = basis_tables(lax.axis_index("blk"), lax.axis_index("win"))
    parts = image_of(
        halo,
        table,
        last,
        cross,
        jnp.asarray(inverse_table()),
        jnp.asarray(spread_table()),
        fine,
        coarse,
    )
    parts = lax.all_to_all(parts, "blk", 0, 0, tiled=True)
    return gather(parts, jnp.asarray(gather_table()))


def solution(mesh):
    segments = mesh.shape["fibre"] // SEG_BLOCKS
    inner = Mesh(
        mesh.devices.reshape(segments, SEG_BLOCKS, mesh.shape["win"]), ("seg", "blk", "win")
    )
    placed = (P("win", None, ("seg", "blk")), P(("seg", "blk")))
    return jax.shard_map(
        local, mesh=inner, in_specs=placed, out_specs=P(("seg", "blk"), "win"), check_vma=False
    )
```

time: 66.3 us -> 56.9 us (0.86)
  local copies, waits for them, and re-layouts: 5.17 us -> 0.03 us
  other arithmetic: 3.77 us -> 1.39 us
  Pallas kernels: 9.03 us -> 8.05 us
    unnamed x18 -> x8, local copies, waits for them, and re-layouts: 4.65 us -> 0.02 us
    concatenate x1, other arithmetic: 1.01 us -> 0.06 us  [basis_tables(): fine_table = jnp.concatenate([fine_cos, fine_sin], axis=1).astype(BF16)]
    all_to_all x1, waiting for transfers between devices: 15.1 us -> 14.3 us  [local(): received = lax.all_to_all(whitened, ('blk', 'win'), 0, 0, tiled=True)]
    all_to_all x1 -> x0, other arithmetic: 0.72 us -> none  [local(): parts = lax.all_to_all(parts, 'blk', 0, 0, tiled=True)]
    sub x1, other arithmetic: 1.94 us -> 1.23 us  [turn_waves(): return (1.0 - 2.0 * sine * sine, 2.0 * sine * cosine)]
  transfers between devices with their start and end apart: 2 -> 2, of which waited for: 2 -> 2; matrix products, arithmetic and copies ran while one was open for 5% -> 2% of each run, Pallas kernels for 3% -> 4%
where the time goes in v2:
time: 56.9 us; the launch traced here: 56.7 us
  starting transfers between devices  19.5 us (34%)
  waiting for transfers between devices  18 us (32%)
  blocking collectives  8.72 us (15%)
  Pallas kernels  8.05 us (14%)
  other arithmetic  1.39 us (2%)
  matrix products  0.88 us (2%)
    all_to_all x1, waiting for transfers between devices, local(): received = lax.all_to_all(whitened, ('blk', 'win'), 0, 0, tiled=True)  14.3 us
    ppermute x1, starting transfers between devices, local(): lax.ppermute(first_block, 'seg', [(s, s - 1) for s in range(1, segments)])  11.7 us
    all_to_all x1, blocking collectives, local(): parts = lax.all_to_all(parts, 'blk', 0, 0, tiled=True)  8.72 us
    all_to_all x1, starting transfers between devices, local(): received = lax.all_to_all(whitened, ('blk', 'win'), 0, 0, tiled=True)  7.78 us
    pallas_call x1, Pallas kernels, whiten(): pl.pallas_call(whiten_kernel, in_specs=[pl.BlockSpec(memory_space=pl.ANY)...  4.55 us
    ppermute x1, waiting for transfers between devices, local(): lax.ppermute(first_block, 'seg', [(s, s - 1) for s in range(1, segments)])  3.67 us
    pallas_call x1, Pallas kernels, own_products(): pl.pallas_call(own_kernel, out_shape=(jax.ShapeDtypeStruct((GROUP, 2 * WA...  2.04 us
    pallas_call x1, Pallas kernels, image_of(): pl.pallas_call(image_kernel, out_shape=jax.ShapeDtypeStruct((SEG_BLOCKS,...  1.47 us
  transfers between devices with their start and end apart: 2, of which 2 were waited for; matrix products, arithmetic and copies ran while one was open for 2% of the time, Pallas kernels for 4%

profile of v2, /device:TPU:8, one launch (start us, length us, event | category | flops | bytes accessed | tf_op | source)
XLA Modules:
  0.0 56.7 jit_solution(13699381029427188480)
XLA Ops:
  0.0 4.5 %whiten.1 = bf16[32,56,256]{2,1,0:T(8,128)(2,1)} custom-call(bf16[2,2000,256]{2,1,0:T(8,128)(2,1)} %samples_hbm.1, bf16[4,896,256]{2,1,0:T(8,128)(2,1)} %constant.118.clone.table_hbm, f32[1,256]{1,0:T(1,128)} %bitcast.4), custom_call_target="tpu_custom_call" | custom-call | flops 1835008000 | bytes 5242880 | tf_op jit(solution)/shard_map/whiten/pallas_call | solution.py:266
  4.6 7.8 %all-to-all-start = ((bf16[32,56,256]{2,1,0:T(8,128)(2,1)}), bf16[32,56,256]{2,1,0:T(8,128)(2,1)S(1)}, u32[]{:S(2)}, u32[]{:S(2)}) async-start(bf16[32,56,256]{2,1,0:T(8,128)(2,1)} %whiten.1), calls=%async_computation | async-start | bytes 1835008 | tf_op jit(solution)/shard_map/all_to_all | solution.py:475
  12.4 1.2 %fusion.3 = (f32[256,512]{1,0:T(8,128)S(1)}, f32[256,512]{1,0:T(8,128)S(1)}, bf16[256,512]{1,0:T(8,128)(2,1)S(1)}, bf16[256,512]{1,0:T(8,128)(2,1)S(1)}) fusion(f32[512]{0:T(512)S(1)} %add_divide_fusion, f32[256]{0:T(256)S(1)} %get-tuple-element.15, f32[256]{0:T(256)S(1)} %get-tuple-element.16), kind=kLoop, calls=%fused_computation.10 | loop fusion | flops 8650752 | bytes 1576960 | tf_op jit(solution)/shard_map/sub | solution.py:136
  13.6 0.0 copy-start
  13.6 0.1 pad_maximum_fusion.coarse_ref
  13.7 14.3 %all-to-all-done.recv_ref = bf16[32,56,256]{2,1,0:T(8,128)(2,1)S(1)} async-done(((bf16[32,56,256]{2,1,0:T(8,128)(2,1)}), bf16[32,56,256]{2,1,0:T(8,128)(2,1)S(1)}, u32[]{:S(2)}, u32[]{:S(2)}) %all-to-all-start) | async-done | bytes 917536 | tf_op jit(solution)/shard_map/all_to_all | solution.py:475
  28.1 11.7 %collective-permute-start = (bf16[4,56,256]{2,1,0:T(8,128)(2,1)S(1)}, bf16[4,56,256]{2,1,0:T(8,128)(2,1)S(1)}, u32[]{:S(2)}, u32[]{:S(2)}) collective-permute-start(bf16[4,56,256]{2,1,0:T(8,128)(2,1)S(1)} %slice.9), channel_id=1, source_target_pairs={{32,0},{64,32},{96,64},{128,96},{160,128},{192,160},{224,192},{256... | collective-permute-start | bytes 344072 | tf_op jit(solution)/shard_map/ppermute | solution.py:478
  39.8 0.1 pad_maximum_fusion.1.fine_ref
  39.9 0.0 copy-done
  39.9 0.0 copy-start.1
  39.9 0.0 copy-start.2
  39.9 2.0 %own_products.1 = (f32[128,1024]{1,0:T(8,128)S(1)}, f32[32,1024]{1,0:T(8,128)S(1)}) custom-call(bf16[32,56,256]{2,1,0:T(8,128)(2,1)S(1)} %all-to-all-done.recv_ref, bf16[512,1024]{1,0:T(8,128)(2,1)S(1)} %copy-done), custom_call_target="tpu_custom_call" | custom-call | flops 1073741824 | bytes 8388608 | tf_op jit(solution)/shard_map/own_products/pallas_call | solution.py:349
  41.9 3.7 %collective-permute-done.halo_ref = bf16[4,56,256]{2,1,0:T(8,128)(2,1)S(1)} collective-permute-done((bf16[4,56,256]{2,1,0:T(8,128)(2,1)S(1)}, bf16[4,56,256]{2,1,0:T(8,128)(2,1)S(1)}, u32[]{:S(2)}, u32[]{:S(2)}) %collective-permute-start) | collective-permute-done | bytes 114720 | tf_op jit(solution)/shard_map/ppermute | solution.py:478
  45.6 0.0 copy-done.1
  45.6 0.0 copy-done.2
  45.6 0.0 copy-start.3
  45.6 1.5 %image.1 = f32[8,16,128]{2,1,0:T(8,128)S(1)} custom-call(bf16[4,56,256]{2,1,0:T(8,128)(2,1)S(1)} %collective-permute-done.halo_ref, bf16[512,1024]{1,0:T(8,128)(2,1)S(1)} %copy-done, f32[128,1024]{1,0:T(8,128)S(1)} %get-tuple-element.7.last_ref, f32[32,1024]{1,0:T(8,128)S(1)} %get-tuple-element.8.cross_ref, bf16[1024,512]{1,0:T(8,128)(2,1)S(1)} %copy-done.1, ...), custom_call_target="tpu_custom_call" | custom-call | flops 734003200 | bytes 6291456 | tf_op jit(solution)/shard_map/image/pallas_call | solution.py:448
  47.1 8.7 %all_to_all.10 = f32[8,16,128]{2,1,0:T(8,128)S(1)} all-to-all(f32[8,16,128]{2,1,0:T(8,128)S(1)} %image.1), channel_id=1, replica_groups=mesh['seg'=16,'blk'=8,'win'=4] {'blk'}, dimensions={0} | all-to-all | bytes 131072 | tf_op jit(solution)/shard_map/all_to_all | solution.py:492
  55.8 0.0 copy-done.3
  55.8 0.9 %fusion.12 = f32[64,100]{1,0:T(8,128)} fusion(f32[128,100]{1,0:T(8,128)S(1)} %copy-done.3, f32[128,128]{1,0:T(8,128)S(1)} %bitcast.3), kind=kOutput, calls=%fused_computation.28 | convolution fusion | flops 9830400 | bytes 142336 | tf_op jit(solution)/shard_map/dot_general | solution.py:463
  (3 shorter events, 0.0 us)
Async XLA Ops:
  4.6 23.5 %all-to-all-start = ((bf16[32,56,256]{2,1,0:T(8,128)(2,1)}), bf16[32,56,256]{2,1,0:T(8,128)(2,1)S(1)}, u32[]{:S(2)}, u32[]{:S(2)}) async-start(bf16[32,56,256]{2,1,0:T(8,128)(2,1)} %whiten.1), calls=%async_computation | async-start | bytes 1835008 | tf_op jit(solution)/shard_map/all_to_all | solution.py:475
  13.6 26.2 %copy-start = (bf16[512,1024]{1,0:T(8,128)(2,1)S(1)}, bf16[512,1024]{1,0:T(8,128)(2,1)}, u32[]{:S(2)}) copy-start(bf16[512,1024]{1,0:T(8,128)(2,1)} %constant.119.clone.table_ref) | copy-start | bytes 3145732
  28.1 17.6 %collective-permute-start = (bf16[4,56,256]{2,1,0:T(8,128)(2,1)S(1)}, bf16[4,56,256]{2,1,0:T(8,128)(2,1)S(1)}, u32[]{:S(2)}, u32[]{:S(2)}) collective-permute-start(bf16[4,56,256]{2,1,0:T(8,128)(2,1)S(1)} %slice.9), channel_id=1, source_target_pairs={{32,0},{64,32},{96,64},{128,96},{160,128},{192,160},{224,192},{256... | collective-permute-start | bytes 344072 | tf_op jit(solution)/shard_map/ppermute | solution.py:478
  39.9 5.7 %copy-start.1 = (bf16[1024,512]{1,0:T(8,128)(2,1)S(1)}, bf16[1024,512]{1,0:T(8,128)(2,1)}, u32[]{:S(2)}) copy-start(bf16[1024,512]{1,0:T(8,128)(2,1)} %constant.120.clone.lead_ref) | copy-start | bytes 3145732
  39.9 5.7 %copy-start.2 = (bf16[256,256]{1,0:T(8,128)(2,1)S(1)}, bf16[256,256]{1,0:T(8,128)(2,1)}, u32[]{:S(2)}) copy-start(bf16[256,256]{1,0:T(8,128)(2,1)} %constant.121.clone.spread_ref) | copy-start | bytes 393220
  45.6 10.2 %copy-start.3 = (f32[128,100]{1,0:T(8,128)S(1)}, f32[128,100]{1,0:T(8,128)}, u32[]{:S(2)}) copy-start(f32[128,100]{1,0:T(8,128)} %constant.122.clone) | copy-start | bytes 153604

commit v3 on v2

--- a/solution.py
+++ b/solution.py
@@ -19,18 +19,18 @@
 WIN_DEVICES = 4
 DESTS = SEG_BLOCKS * WIN_DEVICES
 CHUNK = FREQS // WIN_DEVICES
-FIRST_BIN = [0, 12, 26, 38, 50, 62, 76, 88, CHUNK]
+FIRST_BIN = [0, 13, 25, 38, 50, 63, 75, 88, CHUNK]
 SLOT = 16
 TILE = 8
-SENT = 7 * TILE
+SENT = 13 * TILE
 TAKEN = 4 * TILE
 LOCAL_WINDOWS = 2
 DIGIT = 16
-ROWS = DESTS // 2 * SENT
+ROWS = SEG_BLOCKS * 13 * TILE
+LANES = 128
 STEP = 256
 STEPS = 4
 HALF = SAMPLES // 2
-LANES = 128
 BF16 = jnp.bfloat16
 F32 = jnp.float32
 
@@ -43,18 +43,15 @@
 
 def table_rows():
     bins, parts = [], []
-    for pair in range(DESTS // 2):
-        dests = [bins_of(d // WIN_DEVICES, d % WIN_DEVICES) for d in (2 * pair, 2 * pair + 1)]
-        own = []
+    for block in range(SEG_BLOCKS):
+        dests = [bins_of(block, window_device) for window_device in range(WIN_DEVICES)]
+        rows = []
         for dest in dests:
-            own.append(
-                [(dest[r], 0) for r in range(8)]
-                + [(dest[r], 1) for r in range(8)]
-                + [(dest[r], 0) for r in range(8, 12)]
-                + [(dest[r], 1) for r in range(8, 12)]
-            )
-        mixed = [(dest[r], part) for part in (0, 1) for dest in dests for r in (12, 13)]
-        for at, part in own[0] + mixed + own[1]:
+            for first, last in ((0, 8), (8, 12)):
+                for part in (0, 1):
+                    rows += [(dest[r], part) for r in range(first, last)]
+        rows += [(dest[12], part) for part in (0, 1) for dest in dests]
+        for at, part in rows:
             bins.append(at)
             parts.append(part)
     return np.array(bins), np.array(parts)
@@ -140,7 +137,7 @@
     speeds = jnp.arange(VEL, dtype=jnp.int32)
     speed = 150.0 + 1350.0 * speeds.astype(F32) / (VEL - 1)
     slowness = (200.0 * 8.0 / SAMPLES / speed)[None, :]
-    first = window_device * CHUNK + (25 * block + 2) // 4 * 2 + 1
+    first = window_device * CHUNK + (25 * block + 1) // 2 + 1
     index = jnp.arange(SLOT * DIGIT, dtype=jnp.int32)
     fine = ((first + index // DIGIT) * (index % DIGIT)).astype(F32)[:, None]
     coarse = ((first + index % SLOT) * (index // SLOT * DIGIT)).astype(F32)[:, None]
@@ -192,11 +189,13 @@
             copy.start()
     weights_copy.start()
 
-    row = lax.broadcasted_iota(jnp.int32, (SLOT, STEP), 0)
-    sign = jnp.where(row % 2 == 0, -1.0, 1.0).astype(BF16)
+    row = lax.broadcasted_iota(jnp.int32, (ROWS // SEG_BLOCKS, STEP), 0)
+    odd = jnp.where((row % 2 == 0) | (row >= 12 * TILE), -1.0, 1.0)
+    sign = jnp.concatenate(
+        [odd if FIRST_BIN[block] % 2 == 0 else -odd for block in range(SEG_BLOCKS)], axis=0
+    ).astype(BF16)
     tile_row = lax.broadcasted_iota(jnp.int32, (TILE, OFFS), 0)
     upper_half = tile_row < 4
-    upper_pair = tile_row % 4 < 2
     missing = HALF - (STEPS - 1) * STEP + 8
     late_ref[STEPS - 1, :, missing:, :] = jnp.zeros(
         (LOCAL_WINDOWS, STEP + 16 - missing, OFFS), BF16
@@ -206,7 +205,7 @@
         for copy in copies[step]:
             copy.wait()
         table = table_ref[step]
-        turned = (table.reshape(ROWS // SLOT, SLOT, STEP) * sign[None]).reshape(ROWS, STEP)
+        turned = table * sign
         pair = jnp.concatenate([table, turned], axis=1)
         samples = jnp.concatenate(
             [
@@ -232,26 +231,42 @@
     done = []
     for part in range(OUT_PARTS):
         first = part * (DESTS // OUT_PARTS)
-        for pair in range(first // 2, (first + DESTS // OUT_PARTS) // 2):
+        for block in range(first // WIN_DEVICES, (first + DESTS // OUT_PARTS) // WIN_DEVICES):
+            rows = slice(block * 13 * TILE, (block + 1) * 13 * TILE)
             values = [
-                raw_ref[pair * SENT : (pair + 1) * SENT, w * OFFS : (w + 1) * OFFS] * factors[w]
+                raw_ref[rows, w * OFFS : (w + 1) * OFFS] * factors[w]
                 for w in range(LOCAL_WINDOWS)
             ]
-            mixed = [value[3 * TILE : 4 * TILE] for value in values]
-            for odd in range(2):
-                one, two = [value[4 * odd * TILE : (4 * odd + 3) * TILE] for value in values]
+            final = [value[12 * TILE :] for value in values]
+            for dest in range(WIN_DEVICES):
+                one, two = [
+                    value[3 * dest * TILE : 3 * (dest + 1) * TILE] for value in values
+                ]
                 ends = [one[2 * TILE :], two[2 * TILE :]]
-                pieces = [
-                    one[: 2 * TILE],
-                    two[: 2 * TILE],
-                    jnp.where(upper_half, ends[0], pltpu.roll(ends[1], 4, 0)),
-                    jnp.where(upper_half, pltpu.roll(ends[0], 4, 0), ends[1]),
+                six = jnp.concatenate(
+                    [
+                        one[: 2 * TILE],
+                        two[: 2 * TILE],
+                        jnp.where(upper_half, ends[0], pltpu.roll(ends[1], 4, 0)),
+                        jnp.where(upper_half, pltpu.roll(ends[0], 4, 0), ends[1]),
+                    ],
+                    axis=0,
+                )
+                moved = [
+                    pltpu.roll(final[at % 2], (at - at // 2 * 4 - dest) % TILE, 0)
+                    for at in range(4)
                 ]
-                if odd == 0:
-                    pieces.append(jnp.where(upper_pair, mixed[0], pltpu.roll(mixed[1], 2, 0)))
-                else:
-                    pieces.append(jnp.where(upper_pair, pltpu.roll(mixed[0], 6, 0), mixed[1]))
-                out_ref[2 * pair + odd] = jnp.concatenate(pieces, axis=0).astype(BF16)
+                mixed = moved[3]
+                for at in range(3):
+                    mixed = jnp.where(tile_row == at, moved[at], mixed)
+                mixed = jnp.where(
+                    upper_half[:, :LANES],
+                    mixed[:, :LANES],
+                    pltpu.roll(mixed[:, LANES:], 4, 0),
+                )
+                out_ref[block * WIN_DEVICES + dest] = jnp.concatenate(
+                    [six[:, :LANES], six[:, LANES:], mixed], axis=0
+                ).astype(BF16)
         here = pl.ds(first, DESTS // OUT_PARTS)
         done.append(pltpu.make_async_copy(out_ref.at[here], out_hbm.at[here], out_sems.at[part]))
         done[-1].start()
@@ -267,14 +282,14 @@
         whiten_kernel,
         in_specs=[pl.BlockSpec(memory_space=pl.ANY)] * 3,
         out_specs=pl.BlockSpec(memory_space=pl.ANY),
-        out_shape=jax.ShapeDtypeStruct((DESTS, SENT, OFFS), BF16),
+        out_shape=jax.ShapeDtypeStruct((DESTS, SENT, LANES), BF16),
         scratch_shapes=[
             pltpu.VMEM((STEPS, LOCAL_WINDOWS, STEP, OFFS), BF16),
             pltpu.VMEM((STEPS, LOCAL_WINDOWS, STEP + 16, OFFS), BF16),
             pltpu.VMEM((STEPS, ROWS, STEP), BF16),
             pltpu.VMEM((1, OFFS), F32),
             pltpu.VMEM((ROWS, LOCAL_WINDOWS * OFFS), F32),
-            pltpu.VMEM((DESTS, SENT, OFFS), BF16),
+            pltpu.VMEM((DESTS, SENT, LANES), BF16),
             pltpu.SemaphoreType.DMA((3 * STEPS + 1,)),
             pltpu.SemaphoreType.DMA((OUT_PARTS,)),
         ],
@@ -292,11 +307,13 @@
 
 def side_by_side(slot):
     values = slot.astype(F32)
-    tiles = [values[at * TILE : (at + 1) * TILE] for at in range(7)]
-    real = jnp.concatenate([tiles[0], tiles[2], tiles[4], tiles[6]], axis=0)
-    imag = jnp.concatenate(
-        [tiles[1], tiles[3], tiles[5], pltpu.roll(tiles[6], 4, 0)], axis=0
-    )
+    six = jnp.concatenate([values[: 6 * TILE], values[6 * TILE : 12 * TILE]], axis=1)
+    tiles = [six[at * TILE : (at + 1) * TILE] for at in range(6)]
+    mixed = values[12 * TILE :]
+    real = jnp.concatenate([mixed, pltpu.roll(mixed, 4, 0)], axis=1)
+    imag = jnp.concatenate([pltpu.roll(mixed, 6, 0), pltpu.roll(mixed, 2, 0)], axis=1)
+    real = jnp.concatenate([tiles[0], tiles[2], tiles[4], real], axis=0)
+    imag = jnp.concatenate([tiles[1], tiles[3], tiles[5], imag], axis=0)
     return jnp.concatenate([real, imag], axis=1).astype(BF16)
 
 
@@ -304,8 +321,8 @@
     tile_row = lax.broadcasted_iota(jnp.int32, (TILE, values.shape[1]), 0)
     tiles = [values[at * TILE : (at + 1) * TILE] for at in range(4)]
     four = tiles[2] + pltpu.roll(tiles[2], 4, 0)
-    two = pltpu.roll(tiles[3] + pltpu.roll(tiles[3], 6, 0), 4, 0)
-    rest = jnp.where(tile_row < 4, four, jnp.where(tile_row < 6, two, 0.0))
+    one = pltpu.roll(tiles[3] + pltpu.roll(tiles[3], 7, 0), 4, 0)
+    rest = jnp.where(tile_row < 4, four, jnp.where(tile_row == 4, one, 0.0))
     return jnp.concatenate([tiles[0] + tiles[1], rest], axis=0)
 
 

time: 56.9 us -> 55.4 us (0.974)
  waiting for transfers between devices: 18 us -> 16.6 us
    all_to_all x1, waiting for transfers between devices: 14.3 us -> 13.5 us  [local(): received = lax.all_to_all(whitened, ('blk', 'win'), 0, 0, tiled=True)]
    ppermute x1, waiting for transfers between devices: 3.67 us -> 3.03 us  [local(): lax.ppermute(first_block, 'seg', [(s, s - 1) for s in range(1, segments)])]
  transfers between devices with their start and end apart: 2 -> 2, of which waited for: 2 -> 2; matrix products, arithmetic and copies ran while one was open for 2% -> 3% of each run, Pallas kernels for 4% -> 4%
where the time goes in v3:
time: 55.4 us; the launch traced here: 55.1 us
  starting transfers between devices  19.5 us (35%)
  waiting for transfers between devices  16.6 us (30%)
  blocking collectives  8.72 us (16%)
  Pallas kernels  7.91 us (14%)
  other arithmetic  1.39 us (3%)
  matrix products  0.88 us (2%)
    all_to_all x1, waiting for transfers between devices, local(): received = lax.all_to_all(whitened, ('blk', 'win'), 0, 0, tiled=True)  13.5 us
    ppermute x1, starting transfers between devices, local(): lax.ppermute(first_block, 'seg', [(s, s - 1) for s in range(1, segments)])  11.7 us
    all_to_all x1, blocking collectives, local(): parts = lax.all_to_all(parts, 'blk', 0, 0, tiled=True)  8.72 us
    all_to_all x1, starting transfers between devices, local(): received = lax.all_to_all(whitened, ('blk', 'win'), 0, 0, tiled=True)  7.78 us
    pallas_call x1, Pallas kernels, whiten(): pl.pallas_call(whiten_kernel, in_specs=[pl.BlockSpec(memory_space=pl.ANY)...  4.39 us
    ppermute x1, waiting for transfers between devices, local(): lax.ppermute(first_block, 'seg', [(s, s - 1) for s in range(1, segments)])  3.03 us
    pallas_call x1, Pallas kernels, own_products(): pl.pallas_call(own_kernel, out_shape=(jax.ShapeDtypeStruct((GROUP, 2 * WA...  2.04 us
    pallas_call x1, Pallas kernels, image_of(): pl.pallas_call(image_kernel, out_shape=jax.ShapeDtypeStruct((SEG_BLOCKS,...  1.48 us
  transfers between devices with their start and end apart: 2, of which 2 were waited for; matrix products, arithmetic and copies ran while one was open for 3% of the time, Pallas kernels for 4%

profile of v3, /device:TPU:8, one launch (start us, length us, event | category | flops | bytes accessed | tf_op | source)
XLA Modules:
  0.0 55.1 jit_solution(8477352921138636881)
XLA Ops:
  0.0 4.4 %whiten.1 = bf16[32,104,128]{2,1,0:T(8,128)(2,1)} custom-call(bf16[2,2000,256]{2,1,0:T(8,128)(2,1)} %samples_hbm.1, bf16[4,832,256]{2,1,0:T(8,128)(2,1)} %constant.115.clone.table_hbm, f32[1,256]{1,0:T(1,128)} %bitcast.4), custom_call_target="tpu_custom_call" | custom-call | flops 1703936000 | bytes 5242880 | tf_op jit(solution)/shard_map/whiten/pallas_call | solution.py:281
  4.4 7.8 %all-to-all-start = ((bf16[32,104,128]{2,1,0:T(8,128)(2,1)}), bf16[32,104,128]{2,1,0:T(8,128)(2,1)S(1)}, u32[]{:S(2)}, u32[]{:S(2)}) async-start(bf16[32,104,128]{2,1,0:T(8,128)(2,1)} %whiten.1), calls=%async_computation | async-start | bytes 1703936 | tf_op jit(solution)/shard_map/all_to_all | solution.py:492
  12.2 1.2 %fusion.3 = (f32[256,512]{1,0:T(8,128)S(1)}, f32[256,512]{1,0:T(8,128)S(1)}, bf16[256,512]{1,0:T(8,128)(2,1)S(1)}, bf16[256,512]{1,0:T(8,128)(2,1)S(1)}) fusion(f32[512]{0:T(512)S(1)} %add_divide_fusion, f32[256]{0:T(256)S(1)} %get-tuple-element.15, f32[256]{0:T(256)S(1)} %get-tuple-element.16), kind=kLoop, calls=%fused_computation.10 | loop fusion | flops 8650752 | bytes 1576960 | tf_op jit(solution)/shard_map/sub | solution.py:133
  13.5 0.0 copy-start
  13.5 0.1 pad_maximum_fusion.coarse_ref
  13.6 13.5 %all-to-all-done.recv_ref = bf16[32,104,128]{2,1,0:T(8,128)(2,1)S(1)} async-done(((bf16[32,104,128]{2,1,0:T(8,128)(2,1)}), bf16[32,104,128]{2,1,0:T(8,128)(2,1)S(1)}, u32[]{:S(2)}, u32[]{:S(2)}) %all-to-all-start) | async-done | bytes 852000 | tf_op jit(solution)/shard_map/all_to_all | solution.py:492
  27.1 11.7 %collective-permute-start = (bf16[4,104,128]{2,1,0:T(8,128)(2,1)S(1)}, bf16[4,104,128]{2,1,0:T(8,128)(2,1)S(1)}, u32[]{:S(2)}, u32[]{:S(2)}) collective-permute-start(bf16[4,104,128]{2,1,0:T(8,128)(2,1)S(1)} %slice.9), channel_id=1, source_target_pairs={{32,0},{64,32},{96,64},{128,96},{160,128},{192,160},{224,192},{256... | collective-permute-start | bytes 319496 | tf_op jit(solution)/shard_map/ppermute | solution.py:495
  38.9 0.1 pad_maximum_fusion.1.fine_ref
  38.9 0.0 copy-done
  38.9 0.0 copy-start.1
  38.9 0.0 copy-start.2
  39.0 2.0 %own_products.1 = (f32[128,1024]{1,0:T(8,128)S(1)}, f32[32,1024]{1,0:T(8,128)S(1)}) custom-call(bf16[32,104,128]{2,1,0:T(8,128)(2,1)S(1)} %all-to-all-done.recv_ref, bf16[512,1024]{1,0:T(8,128)(2,1)S(1)} %copy-done), custom_call_target="tpu_custom_call" | custom-call | flops 1073741824 | bytes 8388608 | tf_op jit(solution)/shard_map/own_products/pallas_call | solution.py:366
  41.0 3.0 %collective-permute-done.halo_ref = bf16[4,104,128]{2,1,0:T(8,128)(2,1)S(1)} collective-permute-done((bf16[4,104,128]{2,1,0:T(8,128)(2,1)S(1)}, bf16[4,104,128]{2,1,0:T(8,128)(2,1)S(1)}, u32[]{:S(2)}, u32[]{:S(2)}) %collective-permute-start) | collective-permute-done | bytes 106528 | tf_op jit(solution)/shard_map/ppermute | solution.py:495
  44.0 0.0 copy-done.1
  44.0 0.0 copy-done.2
  44.0 0.0 copy-start.3
  44.0 1.5 %image.1 = f32[8,16,128]{2,1,0:T(8,128)S(1)} custom-call(bf16[4,104,128]{2,1,0:T(8,128)(2,1)S(1)} %collective-permute-done.halo_ref, bf16[512,1024]{1,0:T(8,128)(2,1)S(1)} %copy-done, f32[128,1024]{1,0:T(8,128)S(1)} %get-tuple-element.7.last_ref, f32[32,1024]{1,0:T(8,128)S(1)} %get-tuple-element.8.cross_ref, bf16[1024,512]{1,0:T(8,128)(2,1)S(1)} %copy-done.1, ...), custom_call_target="tpu_custom_call" | custom-call | flops 734003200 | bytes 6291456 | tf_op jit(solution)/shard_map/image/pallas_call | solution.py:465
  45.5 8.7 %all_to_all.10 = f32[8,16,128]{2,1,0:T(8,128)S(1)} all-to-all(f32[8,16,128]{2,1,0:T(8,128)S(1)} %image.1), channel_id=1, replica_groups=mesh['seg'=16,'blk'=8,'win'=4] {'blk'}, dimensions={0} | all-to-all | bytes 131072 | tf_op jit(solution)/shard_map/all_to_all | solution.py:509
  54.2 0.0 copy-done.3
  54.3 0.9 %fusion.12 = f32[64,100]{1,0:T(8,128)} fusion(f32[128,100]{1,0:T(8,128)S(1)} %copy-done.3, f32[128,128]{1,0:T(8,128)S(1)} %bitcast.3), kind=kOutput, calls=%fused_computation.28 | convolution fusion | flops 9830400 | bytes 142336 | tf_op jit(solution)/shard_map/dot_general | solution.py:480
  (3 shorter events, 0.0 us)
Async XLA Ops:
  4.4 22.7 %all-to-all-start = ((bf16[32,104,128]{2,1,0:T(8,128)(2,1)}), bf16[32,104,128]{2,1,0:T(8,128)(2,1)S(1)}, u32[]{:S(2)}, u32[]{:S(2)}) async-start(bf16[32,104,128]{2,1,0:T(8,128)(2,1)} %whiten.1), calls=%async_computation | async-start | bytes 1703936 | tf_op jit(solution)/shard_map/all_to_all | solution.py:492
  13.5 25.5 %copy-start = (bf16[512,1024]{1,0:T(8,128)(2,1)S(1)}, bf16[512,1024]{1,0:T(8,128)(2,1)}, u32[]{:S(2)}) copy-start(bf16[512,1024]{1,0:T(8,128)(2,1)} %constant.116.clone.table_ref) | copy-start | bytes 3145732
  27.1 16.9 %collective-permute-start = (bf16[4,104,128]{2,1,0:T(8,128)(2,1)S(1)}, bf16[4,104,128]{2,1,0:T(8,128)(2,1)S(1)}, u32[]{:S(2)}, u32[]{:S(2)}) collective-permute-start(bf16[4,104,128]{2,1,0:T(8,128)(2,1)S(1)} %slice.9), channel_id=1, source_target_pairs={{32,0},{64,32},{96,64},{128,96},{160,128},{192,160},{224,192},{256... | collective-permute-start | bytes 319496 | tf_op jit(solution)/shard_map/ppermute | solution.py:495
  38.9 5.1 %copy-start.1 = (bf16[1024,512]{1,0:T(8,128)(2,1)S(1)}, bf16[1024,512]{1,0:T(8,128)(2,1)}, u32[]{:S(2)}) copy-start(bf16[1024,512]{1,0:T(8,128)(2,1)} %constant.117.clone.lead_ref) | copy-start | bytes 3145732
  38.9 5.1 %copy-start.2 = (bf16[256,256]{1,0:T(8,128)(2,1)S(1)}, bf16[256,256]{1,0:T(8,128)(2,1)}, u32[]{:S(2)}) copy-start(bf16[256,256]{1,0:T(8,128)(2,1)} %constant.118.clone.spread_ref) | copy-start | bytes 393220
  44.0 10.2 %copy-start.3 = (f32[128,100]{1,0:T(8,128)S(1)}, f32[128,100]{1,0:T(8,128)}, u32[]{:S(2)}) copy-start(f32[128,100]{1,0:T(8,128)} %constant.119.clone) | copy-start | bytes 153604

commit v4 on v3

--- a/solution.py
+++ b/solution.py
@@ -72,13 +72,12 @@
     return np.concatenate([np.arange(0, 2 * OFFS, 2), np.arange(1, 2 * OFFS, 2)])
 
 
-def forward_table():
+def forward_table(sines_first=False):
     rows = np.arange(OFFS)
     angle = 2.0 * np.pi / (2 * OFFS) * ((rows[:, None] * wave_order()[None, :]) % (2 * OFFS))
-    cosines, sines = np.cos(angle), np.sin(angle)
-    upper = np.concatenate([cosines, -sines], axis=1)
-    lower = np.concatenate([sines, cosines], axis=1)
-    return np.concatenate([upper, lower], axis=0).astype(np.float32).astype(ml_dtypes.bfloat16)
+    halves = [np.cos(angle), np.sin(angle)]
+    table = np.concatenate(halves[::-1] if sines_first else halves, axis=1)
+    return table.astype(np.float32).astype(ml_dtypes.bfloat16)
 
 
 def inverse_table():
@@ -93,7 +92,7 @@
 
 def spread_table():
     index = np.arange(OFFS)
-    same = (index[:, None] % DIGIT) == (index[None, :] % DIGIT)
+    same = (index[:, None] % DIGIT) == (index[None, :] // SLOT)
     return same.astype(ml_dtypes.bfloat16)
 
 
@@ -106,7 +105,7 @@
 
 
 def turn_waves(turns):
-    rest = turns - jnp.round(turns)
+    rest = turns - jnp.floor(turns + 0.5)
     half = rest * math.pi
     square = half * half
     sine = half * (
@@ -133,34 +132,34 @@
     return 1.0 - 2.0 * sine * sine, 2.0 * sine * cosine
 
 
-def basis_tables(block, window_device):
+def turns_of(block, window_device):
     speeds = jnp.arange(VEL, dtype=jnp.int32)
     speed = 150.0 + 1350.0 * speeds.astype(F32) / (VEL - 1)
     slowness = (200.0 * 8.0 / SAMPLES / speed)[None, :]
     first = window_device * CHUNK + (25 * block + 1) // 2 + 1
-    index = jnp.arange(SLOT * DIGIT, dtype=jnp.int32)
-    fine = ((first + index // DIGIT) * (index % DIGIT)).astype(F32)[:, None]
-    coarse = ((first + index % SLOT) * (index // SLOT * DIGIT)).astype(F32)[:, None]
-    fine_cos, fine_sin = turn_waves(fine * slowness)
-    coarse_cos, coarse_sin = turn_waves(coarse * slowness)
-    fine_table = jnp.concatenate([fine_cos, fine_sin], axis=1).astype(BF16)
-    coarse_table = jnp.concatenate([coarse_cos, coarse_sin], axis=1)
-    return fine_table, coarse_table
+    return (first + jnp.arange(SLOT, dtype=jnp.int32)).astype(F32)[:, None] * slowness
+
+
+def powers_of(cosine, sine):
+    now = (jnp.ones_like(cosine), jnp.zeros_like(sine))
+    waves = [now]
+    for _ in range(DIGIT - 1):
+        now = (now[0] * cosine - now[1] * sine, now[1] * cosine + now[0] * sine)
+        waves.append(now)
+    return waves
 
 
 def whiten_kernel(
     samples_hbm,
     table_hbm,
     weights_hbm,
-    out_hbm,
+    out_ref,
     early_ref,
     late_ref,
     table_ref,
     weights_ref,
     raw_ref,
-    out_ref,
     in_sems,
-    out_sems,
 ):
     weights_copy = pltpu.make_async_copy(weights_hbm, weights_ref, in_sems.at[3 * STEPS])
     copies = []
@@ -228,60 +227,49 @@
     for w in range(LOCAL_WINDOWS):
         power = jnp.sum(powers[:, w * OFFS : (w + 1) * OFFS], axis=0, keepdims=True) / FREQS
         factors.append(weights_ref[...] / jnp.sqrt(power + EPS))
-    done = []
-    for part in range(OUT_PARTS):
-        first = part * (DESTS // OUT_PARTS)
-        for block in range(first // WIN_DEVICES, (first + DESTS // OUT_PARTS) // WIN_DEVICES):
-            rows = slice(block * 13 * TILE, (block + 1) * 13 * TILE)
-            values = [
-                raw_ref[rows, w * OFFS : (w + 1) * OFFS] * factors[w]
-                for w in range(LOCAL_WINDOWS)
+    for block in range(SEG_BLOCKS):
+        rows = slice(block * 13 * TILE, (block + 1) * 13 * TILE)
+        values = [
+            raw_ref[rows, w * OFFS : (w + 1) * OFFS] * factors[w]
+            for w in range(LOCAL_WINDOWS)
+        ]
+        final = [value[12 * TILE :] for value in values]
+        for dest in range(WIN_DEVICES):
+            one, two = [
+                value[3 * dest * TILE : 3 * (dest + 1) * TILE] for value in values
             ]
-            final = [value[12 * TILE :] for value in values]
-            for dest in range(WIN_DEVICES):
-                one, two = [
-                    value[3 * dest * TILE : 3 * (dest + 1) * TILE] for value in values
-                ]
-                ends = [one[2 * TILE :], two[2 * TILE :]]
-                six = jnp.concatenate(
-                    [
-                        one[: 2 * TILE],
-                        two[: 2 * TILE],
-                        jnp.where(upper_half, ends[0], pltpu.roll(ends[1], 4, 0)),
-                        jnp.where(upper_half, pltpu.roll(ends[0], 4, 0), ends[1]),
-                    ],
-                    axis=0,
-                )
-                moved = [
-                    pltpu.roll(final[at % 2], (at - at // 2 * 4 - dest) % TILE, 0)
-                    for at in range(4)
-                ]
-                mixed = moved[3]
-                for at in range(3):
-                    mixed = jnp.where(tile_row == at, moved[at], mixed)
-                mixed = jnp.where(
-                    upper_half[:, :LANES],
-                    mixed[:, :LANES],
-                    pltpu.roll(mixed[:, LANES:], 4, 0),
-                )
-                out_ref[block * WIN_DEVICES + dest] = jnp.concatenate(
-                    [six[:, :LANES], six[:, LANES:], mixed], axis=0
-                ).astype(BF16)
-        here = pl.ds(first, DESTS // OUT_PARTS)
-        done.append(pltpu.make_async_copy(out_ref.at[here], out_hbm.at[here], out_sems.at[part]))
-        done[-1].start()
-    for copy in done:
-        copy.wait()
-
-
-OUT_PARTS = 4
+            ends = [one[2 * TILE :], two[2 * TILE :]]
+            six = jnp.concatenate(
+                [
+                    one[: 2 * TILE],
+                    two[: 2 * TILE],
+                    jnp.where(upper_half, ends[0], pltpu.roll(ends[1], 4, 0)),
+                    jnp.where(upper_half, pltpu.roll(ends[0], 4, 0), ends[1]),
+                ],
+                axis=0,
+            )
+            moved = [
+                pltpu.roll(final[at % 2], (at - at // 2 * 4 - dest) % TILE, 0)
+                for at in range(4)
+            ]
+            mixed = moved[3]
+            for at in range(3):
+                mixed = jnp.where(tile_row == at, moved[at], mixed)
+            mixed = jnp.where(
+                upper_half[:, :LANES],
+                mixed[:, :LANES],
+                pltpu.roll(mixed[:, LANES:], 4, 0),
+            )
+            out_ref[block * WIN_DEVICES + dest] = jnp.concatenate(
+                [six[:, :LANES], six[:, LANES:], mixed], axis=0
+            ).astype(BF16)
 
 
 def whiten(samples, weights, table):
     return pl.pallas_call(
         whiten_kernel,
         in_specs=[pl.BlockSpec(memory_space=pl.ANY)] * 3,
-        out_specs=pl.BlockSpec(memory_space=pl.ANY),
+        out_specs=pl.BlockSpec(memory_space=pltpu.VMEM),
         out_shape=jax.ShapeDtypeStruct((DESTS, SENT, LANES), BF16),
         scratch_shapes=[
             pltpu.VMEM((STEPS, LOCAL_WINDOWS, STEP, OFFS), BF16),
@@ -289,9 +277,7 @@
             pltpu.VMEM((STEPS, ROWS, STEP), BF16),
             pltpu.VMEM((1, OFFS), F32),
             pltpu.VMEM((ROWS, LOCAL_WINDOWS * OFFS), F32),
-            pltpu.VMEM((DESTS, SENT, LANES), BF16),
             pltpu.SemaphoreType.DMA((3 * STEPS + 1,)),
-            pltpu.SemaphoreType.DMA((OUT_PARTS,)),
         ],
         compiler_params=pltpu.CompilerParams(vmem_limit_bytes=62 << 20),
         cost_estimate=pl.CostEstimate(
@@ -305,7 +291,7 @@
 WAVES = 2 * OFFS
 
 
-def side_by_side(slot):
+def parts_of(slot):
     values = slot.astype(F32)
     six = jnp.concatenate([values[: 6 * TILE], values[6 * TILE : 12 * TILE]], axis=1)
     tiles = [six[at * TILE : (at + 1) * TILE] for at in range(6)]
@@ -314,7 +300,21 @@
     imag = jnp.concatenate([pltpu.roll(mixed, 6, 0), pltpu.roll(mixed, 2, 0)], axis=1)
     real = jnp.concatenate([tiles[0], tiles[2], tiles[4], real], axis=0)
     imag = jnp.concatenate([tiles[1], tiles[3], tiles[5], imag], axis=0)
-    return jnp.concatenate([real, imag], axis=1).astype(BF16)
+    return real.astype(BF16), imag.astype(BF16)
+
+
+def spectrum(real, imag, table, sines_first=False):
+    both = jnp.dot(
+        jnp.concatenate([real, imag], axis=0), table, preferred_element_type=F32
+    )
+    rows = real.shape[0]
+    of_real, of_imag = both[:rows], both[rows:]
+    cosines, sines = slice(0, WAVES), slice(WAVES, 2 * WAVES)
+    if sines_first:
+        cosines, sines = sines, cosines
+    return jnp.concatenate(
+        [of_real[:, cosines] + of_imag[:, sines], of_imag[:, cosines] - of_real[:, sines]], axis=1
+    )
 
 
 def by_bin(values):
@@ -326,11 +326,11 @@
     return jnp.concatenate([tiles[0] + tiles[1], rest], axis=0)
 
 
-def own_kernel(recv_ref, table_ref, last_ref, cross_ref, slots_ref, waves_ref):
+def own_kernel(recv_ref, table_ref, cross_ref, real_ref, imag_ref, waves_ref):
     for source in range(DESTS):
-        slots_ref[source * TAKEN : (source + 1) * TAKEN] = side_by_side(recv_ref[source])
-    waves_ref[...] = jnp.dot(slots_ref[...], table_ref[...], preferred_element_type=F32)
-    last_ref[...] = waves_ref[(SEG_BLOCKS - 1) * GROUP :, :]
+        rows = slice(source * TAKEN, (source + 1) * TAKEN)
+        real_ref[rows], imag_ref[rows] = parts_of(recv_ref[source])
+    waves_ref[...] = spectrum(real_ref[...], imag_ref[...], table_ref[...])
     for half in range(2):
         real_at = half * OFFS
         imag_at = WAVES + half * OFFS
@@ -365,14 +365,12 @@
 def own_products(received, table):
     return pl.pallas_call(
         own_kernel,
-        out_shape=(
-            jax.ShapeDtypeStruct((GROUP, 2 * WAVES), F32),
-            jax.ShapeDtypeStruct((TAKEN, 2 * WAVES), F32),
-        ),
+        out_shape=jax.ShapeDtypeStruct((TAKEN, 2 * WAVES), F32),
         in_specs=[pl.BlockSpec(memory_space=pltpu.VMEM)] * 2,
-        out_specs=(pl.BlockSpec(memory_space=pltpu.VMEM),) * 2,
+        out_specs=pl.BlockSpec(memory_space=pltpu.VMEM),
         scratch_shapes=[
-            pltpu.VMEM((DESTS * TAKEN, WAVES), BF16),
+            pltpu.VMEM((DESTS * TAKEN, OFFS), BF16),
+            pltpu.VMEM((DESTS * TAKEN, OFFS), BF16),
             pltpu.VMEM((DESTS * TAKEN, 2 * WAVES), F32),
         ],
         compiler_params=pltpu.CompilerParams(vmem_limit_bytes=40 << 20),
@@ -384,28 +382,26 @@
 
 
 def image_kernel(
-    halo_ref,
-    table_ref,
-    last_ref,
-    cross_ref,
-    lead_ref,
-    spread_ref,
-    fine_ref,
-    coarse_ref,
-    out_ref,
+    ahead_ref, behind_ref, last_ref, table_ref, cross_ref, lead_ref, spread_ref, turns_ref, out_ref
 ):
     totals = [
         cross_ref[:, at * OFFS : (at + 1) * OFFS] for at in range(4)
     ]
-    spectra = jnp.concatenate([side_by_side(halo_ref[w]) for w in range(WIN_DEVICES)], axis=0)
-    waves = jnp.dot(spectra, table_ref[...], preferred_element_type=F32)
+    following = ahead_ref[...] + behind_ref[...]
+    slots = [following[w] for w in range(WIN_DEVICES)] + [last_ref[w] for w in range(WIN_DEVICES)]
+    reals, imags = zip(*[parts_of(slot) for slot in slots])
+    waves = spectrum(
+        jnp.concatenate(reals, axis=0), jnp.concatenate(imags, axis=0), table_ref[...], True
+    )
+    last = waves[GROUP:]
+    waves = waves[:GROUP]
     for half in range(2):
         real_at = half * OFFS
         imag_at = WAVES + half * OFFS
         next_real = waves[:, real_at : real_at + OFFS]
         next_imag = waves[:, imag_at : imag_at + OFFS]
-        own_real = last_ref[:, real_at : real_at + OFFS]
-        own_imag = last_ref[:, imag_at : imag_at + OFFS]
+        own_real = last[:, real_at : real_at + OFFS]
+        own_imag = last[:, imag_at : imag_at + OFFS]
         more_real = own_real * next_real + own_imag * next_imag
         more_imag = own_imag * next_real - own_real * next_imag
         more_real = jnp.sum(more_real.reshape(WIN_DEVICES, TAKEN, OFFS), axis=0)
@@ -432,7 +428,7 @@
     row = lax.broadcasted_iota(jnp.int32, (size, OFFS), 0)
     lane = lax.broadcasted_iota(jnp.int32, (size, OFFS), 1)
     same_digit = row // SLOT == lane // DIGIT
-    same_bin = row % SLOT == lane // DIGIT
+    same_bin = row % SLOT == lane % SLOT
 
     def spread(values):
         normed = values * factor
@@ -441,19 +437,22 @@
         moved = jnp.dot(picked, spread_ref[...], preferred_element_type=F32)
         return jnp.where(same_bin, moved, 0.0).astype(BF16)
 
+    turns = turns_ref[...]
+    fine = [jnp.concatenate(pair, axis=1).astype(BF16) for pair in powers_of(*turn_waves(turns))]
     of_both = jnp.dot(
         jnp.concatenate([spread(real), spread(imag)], axis=0),
-        fine_ref[...],
+        jnp.concatenate(fine, axis=0),
         preferred_element_type=F32,
     )
-    part_real = of_both[:size, :VEL] + of_both[size:, VEL:]
-    part_imag = of_both[size:, :VEL] - of_both[:size, VEL:]
-    coarse_cos = coarse_ref[:, :VEL]
-    coarse_sin = coarse_ref[:, VEL:]
-    along = part_real * coarse_cos + part_imag * coarse_sin
-    across = part_imag * coarse_cos - part_real * coarse_sin
-    along = jnp.sum(along.reshape(DIGIT, SLOT, VEL), axis=0)
-    across = jnp.sum(across.reshape(DIGIT, SLOT, VEL), axis=0)
+    along = jnp.zeros((SLOT, VEL), F32)
+    across = jnp.zeros((SLOT, VEL), F32)
+    for at, (cosine, sine) in enumerate(powers_of(*turn_waves(turns * DIGIT))):
+        one = of_both[at * SLOT : (at + 1) * SLOT]
+        two = of_both[size + at * SLOT : size + (at + 1) * SLOT]
+        part_real = one[:, :VEL] + two[:, VEL:]
+        part_imag = two[:, :VEL] - one[:, VEL:]
+        along = along + (part_real * cosine + part_imag * sine)
+        across = across + (part_imag * cosine - part_real * sine)
     image = (along * along + across * across) / OFFS
     here = VEL // SEG_BLOCKS
     for block in range(SEG_BLOCKS):
@@ -461,7 +460,7 @@
         out_ref[block] = pair if block % 2 == 0 else jnp.roll(pair, here, axis=1)
 
 
-def image_of(halo, table, last, cross, lead, spread, fine, coarse):
+def image_of(*arrays):
     return pl.pallas_call(
         image_kernel,
         out_shape=jax.ShapeDtypeStruct((SEG_BLOCKS, SLOT, LANES), F32),
@@ -472,7 +471,7 @@
             flops=2 * 700 * 512 * 1024, bytes_accessed=6 << 20, transcendentals=0
         ),
         name="image",
-    )(halo, table, last, cross, lead, spread, fine, coarse)
+    )(*arrays)
 
 
 def gather(parts, table):
@@ -489,25 +488,50 @@
 
 def local(samples_data, coupling):
     whitened = whiten(samples_data, coupling[None, :], jnp.asarray(time_table()))
-    received = lax.all_to_all(whitened, ("blk", "win"), 0, 0, tiled=True)
     segments = lax.axis_size("seg")
-    first_block = received[:WIN_DEVICES]
-    halo = lax.ppermute(first_block, "seg", [(s, s - 1) for s in range(1, segments)])
+    middle = segments // 2
+    place = (lax.axis_index("blk"), lax.axis_index("win"))
     table = jnp.asarray(forward_table())
-    last, cross = own_products(received, table)
-    fine, coarse = basis_tables(lax.axis_index("blk"), lax.axis_index("win"))
-    parts = image_of(
-        halo,
+
+    def exchange(values):
+        return lax.all_to_all(values, ("blk", "win"), 0, 0, tiled=True)
+
+    before = lax.axis_index("seg") < middle
+    received = lax.cond(before, lambda values: values, exchange, whitened)
+    behind = lax.ppermute(
+        received[:WIN_DEVICES], "seg", [(s, s - 1) for s in range(middle, segments)]
+    )
+    nothing = lax.optimization_barrier(jnp.zeros((TAKEN, 2 * WAVES), F32))
+    received, cross, table = lax.cond(
+        before,
+        lambda values, same, table: (exchange(values), same, table),
+        lambda values, _, table: (values, own_products(values, table), table),
+        received,
+        nothing,
         table,
-        last,
+    )
+    behind, received, cross, table = lax.optimization_barrier((behind, received, cross, table))
+    ahead = lax.ppermute(received[:WIN_DEVICES], "seg", [(s, s - 1) for s in range(1, middle)])
+    cross = lax.cond(
+        before,
+        lambda values, _, table: own_products(values, table),
+        lambda _, same, table: same,
+        received,
+        cross,
+        table,
+    )
+    images = image_of(
+        ahead,
+        behind,
+        received[-WIN_DEVICES:],
+        jnp.asarray(forward_table(sines_first=True)),
         cross,
         jnp.asarray(inverse_table()),
         jnp.asarray(spread_table()),
-        fine,
-        coarse,
-    )
-    parts = lax.all_to_all(parts, "blk", 0, 0, tiled=True)
-    return gather(parts, jnp.asarray(gather_table()))
+        turns_of(*place),
+    )
+    images = lax.all_to_all(images, "blk", 0, 0, tiled=True)
+    return gather(images, jnp.asarray(gather_table()))
 
 
 def solution(mesh):

time: 55.4 us -> 52 us (0.939)
  the two profiles are of different devices: /device:TPU:8 before, /device:TPU:192 now
where the time goes in v4:
time: 52 us; the launch traced here: 51.8 us
  blocking collectives  32.5 us (62%)
  Pallas kernels  8.36 us (16%)
  waiting for transfers between devices  6.72 us (13%)
  starting transfers between devices  2.85 us (5%)
  matrix products  0.88 us (2%)
    all_to_all x1, blocking collectives, exchange(): return lax.all_to_all(values, ('blk', 'win'), 0, 0, tiled=True)  23.4 us
    all_to_all x1, blocking collectives, local(): images = lax.all_to_all(images, 'blk', 0, 0, tiled=True)  9.12 us
    ppermute x1, waiting for transfers between devices, local(): lax.ppermute(received[:WIN_DEVICES], 'seg', [(s, s - 1) for s in range(1,...  6.72 us
    pallas_call x1, Pallas kernels, whiten(): pl.pallas_call(whiten_kernel, in_specs=[pl.BlockSpec(memory_space=pl.ANY)...  3.57 us
    pallas_call x1, Pallas kernels, own_products(): pl.pallas_call(own_kernel, out_shape=jax.ShapeDtypeStruct((TAKEN, 2 * WAV...  3.09 us
    ppermute x1, starting transfers between devices, local(): lax.ppermute(received[:WIN_DEVICES], 'seg', [(s, s - 1) for s in range(1,...  2.05 us
    pallas_call x1, Pallas kernels, image_of(): pl.pallas_call(image_kernel, out_shape=jax.ShapeDtypeStruct((SEG_BLOCKS,...  1.71 us
  transfers between devices with their start and end apart: 2, of which 1 were waited for; matrix products, arithmetic and copies ran while one was open for 0% of the time, Pallas kernels for 6%

profile of v4, /device:TPU:192, one launch (start us, length us, event | category | flops | bytes accessed | tf_op | source)
XLA Modules:
  0.0 51.8 jit_solution(15931719137389685964)
XLA Ops:
  0.0 3.6 %whiten.1 = bf16[32,104,128]{2,1,0:T(8,128)(2,1)S(1)} custom-call(bf16[2,2000,256]{2,1,0:T(8,128)(2,1)} %samples_hbm.1, bf16[4,832,256]{2,1,0:T(8,128)(2,1)} %constant.59.clone.table_hbm, f32[1,256]{1,0:T(1,128)} %bitcast.4), custom_call_target="tpu_custom_call" | custom-call | flops 1703936000 | bytes 5242880 | tf_op jit(solution)/shard_map/whiten/pallas_call | solution.py:269
  3.6 0.0 copy-start.4
  3.6 0.8 %collective-permute-start = (bf16[4,104,128]{2,1,0:T(8,128)(2,1)S(1)}, bf16[4,104,128]{2,1,0:T(8,128)(2,1)S(1)}, u32[]{:S(2)}, u32[]{:S(2)}) collective-permute-start(bf16[4,104,128]{2,1,0:T(8,128)(2,1)S(1)} %slice.17), channel_id=1, source_target_pairs={{256,224},{288,256},{320,288},{352,320},{384,352},{416,384},{448,4... | collective-permute-start | bytes 319496 | tf_op jit(solution)/shard_map/ppermute | solution.py:501
  4.5 0.1 copy-done.4
  4.6 23.4 %conditional.4 = (bf16[32,104,128]{2,1,0:T(8,128)(2,1)S(1)}, f32[32,1024]{1,0:T(8,128)S(1)}) conditional(s32[]{:T(128)} %convert_element_type.19, (bf16[32,104,128]{2,1,0:T(8,128)(2,1)S(1)}, bf16[256,1024]{1,0:T(8,128)(2,1)S(1)}) %tuple.37, (bf16[32,104,128]{2,1,0:T(8,128)(2,1)S(1)}, f32[32,1024]{1,0:T(8,128)S(1)}) %tuple.27), branch_computations={%region_2.0_spmd, %region_3.0_spmd} | conditional | flops 1073741824 | bytes 10092560 | solution.py:505
  4.6 23.4 %all_to_all.14 = bf16[32,104,128]{2,1,0:T(8,128)(2,1)S(1)} all-to-all(bf16[32,104,128]{2,1,0:T(8,128)(2,1)S(1)} %get-tuple-element.28), channel_id=1, replica_groups=mesh['seg'=16,'blk'=8,'win'=4] {'blk','win'}, dimensions={0} | all-to-all | bytes 1703936 | tf_op jit(solution)/shard_map/cond/branch_1_fun/all_to_all | solution.py:497
  28.0 0.0 collective-permute-done.behind_ref
  28.0 0.0 copy-start
  28.0 0.0 copy-start.1
  28.1 0.0 copy-start.2
  28.1 2.1 %collective-permute-start.1 = (bf16[4,104,128]{2,1,0:T(8,128)(2,1)S(1)}, bf16[4,104,128]{2,1,0:T(8,128)(2,1)S(1)}, u32[]{:S(2)}, u32[]{:S(2)}) collective-permute-start(bf16[4,104,128]{2,1,0:T(8,128)(2,1)S(1)} %get-tuple-element.45), channel_id=1, source_target_pairs={{32,0},{64,32},{96,64},{128,96},{160,128},{192,160},{224,192},{33,... | collective-permute-start | bytes 319496 | tf_op jit(solution)/shard_map/ppermute | solution.py:514
  30.1 0.1 broadcast_multiply_fusion.turns_ref
  30.2 3.1 %conditional.5 = (f32[32,1024]{1,0:T(8,128)S(1)}) conditional(s32[]{:T(128)} %convert_element_type.19, f32[32,1024]{1,0:T(8,128)S(1)} %get-tuple-element.42, (bf16[32,104,128]{2,1,0:T(8,128)(2,1)S(1)}, bf16[256,1024]{1,0:T(8,128)(2,1)}) %tuple.29), branch_computations={%region_4.0_spmd, %region_5.0_spmd} | conditional | flops 1073741824 | bytes 8388616 | solution.py:515
  30.2 3.1 %own_products.3 = f32[32,1024]{1,0:T(8,128)S(1)} custom-call(bf16[32,104,128]{2,1,0:T(8,128)(2,1)S(1)} %get-tuple-element.30.recv_ref, bf16[256,1024]{1,0:T(8,128)(2,1)} %get-tuple-element.31.table_ref), custom_call_target="tpu_custom_call" | custom-call | flops 1073741824 | bytes 8388608 | tf_op jit(solution)/shard_map/cond/branch_1_fun/own_products/pallas_call | solution.py:366
  33.3 0.0 copy-start.3
  33.3 6.7 %collective-permute-done.1.ahead_ref = bf16[4,104,128]{2,1,0:T(8,128)(2,1)S(1)} collective-permute-done((bf16[4,104,128]{2,1,0:T(8,128)(2,1)S(1)}, bf16[4,104,128]{2,1,0:T(8,128)(2,1)S(1)}, u32[]{:S(2)}, u32[]{:S(2)}) %collective-permute-start.1) | collective-permute-done | bytes 106528 | tf_op jit(solution)/shard_map/ppermute | solution.py:514
  40.0 0.0 copy-done
  40.0 0.0 copy-done.1
  40.0 0.0 copy-done.2
  40.0 1.7 %image.1 = f32[8,16,128]{2,1,0:T(8,128)S(1)} custom-call(bf16[4,104,128]{2,1,0:T(8,128)(2,1)S(1)} %collective-permute-done.1.ahead_ref, bf16[4,104,128]{2,1,0:T(8,128)(2,1)S(1)} %collective-permute-done.behind_ref, bf16[4,104,128]{2,1,0:T(8,128)(2,1)S(1)} %get-tuple-element.44.last_ref, bf16[256,1024]{1,0:T(8,128)(2,1)S(1)} %copy-done.1, ...), custom_call_target="tpu_custom_call" | custom-call | flops 734003200 | bytes 6291456 | tf_op jit(solution)/shard_map/image/pallas_call | solution.py:464
  41.7 9.1 %all_to_all.15 = f32[8,16,128]{2,1,0:T(8,128)S(1)} all-to-all(f32[8,16,128]{2,1,0:T(8,128)S(1)} %image.1), channel_id=1, replica_groups=mesh['seg'=16,'blk'=8,'win'=4] {'blk'}, dimensions={0} | all-to-all | bytes 131072 | tf_op jit(solution)/shard_map/all_to_all | solution.py:533
  50.9 0.0 copy-done.3
  50.9 0.9 %fusion = f32[64,100]{1,0:T(8,128)} fusion(f32[128,100]{1,0:T(8,128)S(1)} %copy-done.3, f32[128,128]{1,0:T(8,128)S(1)} %bitcast.3), kind=kOutput, calls=%fused_computation | convolution fusion | flops 9830400 | bytes 142336 | tf_op jit(solution)/shard_map/dot_general | solution.py:479
  (6 shorter events, 0.1 us)
Async XLA Ops:
  3.6 1.0 %copy-start.4 = (bf16[256,1024]{1,0:T(8,128)(2,1)S(1)}, bf16[256,1024]{1,0:T(8,128)(2,1)}, u32[]{:S(2)}) copy-start(bf16[256,1024]{1,0:T(8,128)(2,1)} %constant.60.clone) | copy-start | bytes 1572868
  3.6 24.4 %collective-permute-start = (bf16[4,104,128]{2,1,0:T(8,128)(2,1)S(1)}, bf16[4,104,128]{2,1,0:T(8,128)(2,1)S(1)}, u32[]{:S(2)}, u32[]{:S(2)}) collective-permute-start(bf16[4,104,128]{2,1,0:T(8,128)(2,1)S(1)} %slice.17), channel_id=1, source_target_pairs={{256,224},{288,256},{320,288},{352,320},{384,352},{416,384},{448,4... | collective-permute-start | bytes 319496 | tf_op jit(solution)/shard_map/ppermute | solution.py:501
  28.0 12.0 %copy-start = (bf16[1024,512]{1,0:T(8,128)(2,1)S(1)}, bf16[1024,512]{1,0:T(8,128)(2,1)}, u32[]{:S(2)}) copy-start(bf16[1024,512]{1,0:T(8,128)(2,1)} %constant.62.clone.lead_ref) | copy-start | bytes 3145732
  28.0 12.0 %copy-start.1 = (bf16[256,1024]{1,0:T(8,128)(2,1)S(1)}, bf16[256,1024]{1,0:T(8,128)(2,1)}, u32[]{:S(2)}) copy-start(bf16[256,1024]{1,0:T(8,128)(2,1)} %constant.61.clone.table_ref) | copy-start | bytes 1572868
  28.1 12.0 %copy-start.2 = (bf16[256,256]{1,0:T(8,128)(2,1)S(1)}, bf16[256,256]{1,0:T(8,128)(2,1)}, u32[]{:S(2)}) copy-start(bf16[256,256]{1,0:T(8,128)(2,1)} %constant.63.clone.spread_ref) | copy-start | bytes 393220
  28.1 12.0 %collective-permute-start.1 = (bf16[4,104,128]{2,1,0:T(8,128)(2,1)S(1)}, bf16[4,104,128]{2,1,0:T(8,128)(2,1)S(1)}, u32[]{:S(2)}, u32[]{:S(2)}) collective-permute-start(bf16[4,104,128]{2,1,0:T(8,128)(2,1)S(1)} %get-tuple-element.45), channel_id=1, source_target_pairs={{32,0},{64,32},{96,64},{128,96},{160,128},{192,160},{224,192},{33,... | collective-permute-start | bytes 319496 | tf_op jit(solution)/shard_map/ppermute | solution.py:514
  33.3 17.6 %copy-start.3 = (f32[128,100]{1,0:T(8,128)S(1)}, f32[128,100]{1,0:T(8,128)}, u32[]{:S(2)}) copy-start(f32[128,100]{1,0:T(8,128)} %constant.64.clone) | copy-start | bytes 153604

commit v5 on v4

--- a/solution.py
+++ b/solution.py
@@ -83,11 +83,8 @@
 def inverse_table():
     lags = np.arange(OFFS)
     angle = 2.0 * np.pi / (2 * OFFS) * ((wave_order()[:, None] * lags[None, :]) % (2 * OFFS))
-    cosines, sines = np.cos(angle), np.sin(angle)
-    upper = np.concatenate([cosines, -sines], axis=1)
-    lower = np.concatenate([sines, cosines], axis=1)
-    full = (np.concatenate([upper, lower], axis=0) / (2 * OFFS)).astype(np.float32)
-    return full.astype(ml_dtypes.bfloat16)
+    table = np.concatenate([np.cos(angle), np.sin(angle)], axis=1) / (2 * OFFS)
+    return table.astype(np.float32).astype(ml_dtypes.bfloat16)
 
 
 def spread_table():
@@ -412,16 +409,17 @@
     cross = by_bin(jnp.concatenate(totals, axis=1))
     flat_real = jnp.sum(cross[:, :WAVES], axis=1, keepdims=True) / WAVES
     flat_imag = jnp.sum(cross[:, WAVES:], axis=1, keepdims=True) / WAVES
-    cross = jnp.concatenate([cross[:, :WAVES] - flat_real, cross[:, WAVES:] - flat_imag], axis=1)
+    cross = jnp.concatenate([cross[:, :WAVES] - flat_real, cross[:, WAVES:] - flat_imag], axis=0)
     upper = cross.astype(BF16)
     lower = (cross - upper.astype(F32)).astype(BF16)
-    both = jnp.concatenate([upper, lower], axis=0)
-    stack = jnp.dot(both, lead_ref[...], preferred_element_type=F32)
-    stack = stack[:SLOT] + stack[SLOT:]
-    lag = lax.broadcasted_iota(jnp.int32, (SLOT, 2 * OFFS), 1)
-    stack = stack + jnp.where(lag == 0, flat_real, jnp.where(lag == OFFS, flat_imag, 0.0))
-    real = stack[:, :OFFS]
-    imag = stack[:, OFFS:]
+    both = jnp.dot(
+        jnp.concatenate([upper, lower], axis=0), lead_ref[...], preferred_element_type=F32
+    )
+    both = both[: 2 * SLOT] + both[2 * SLOT :]
+    of_real, of_imag = both[:SLOT], both[SLOT:]
+    lag = lax.broadcasted_iota(jnp.int32, (SLOT, OFFS), 1)
+    real = of_real[:, :OFFS] + of_imag[:, OFFS:] + jnp.where(lag == 0, flat_real, 0.0)
+    imag = of_imag[:, :OFFS] - of_real[:, OFFS:] + jnp.where(lag == 0, flat_imag, 0.0)
     power = jnp.sum(real * real + imag * imag, axis=1, keepdims=True) / OFFS
     factor = 1.0 / jnp.sqrt(power + EPS)
     size = SLOT * DIGIT
@@ -430,19 +428,21 @@
     same_digit = row // SLOT == lane // DIGIT
     same_bin = row % SLOT == lane % SLOT
 
-    def spread(values):
+    def repeated(values):
         normed = values * factor
-        repeated = jnp.broadcast_to(normed[None], (DIGIT, SLOT, OFFS)).reshape(size, OFFS)
-        picked = jnp.where(same_digit, repeated, 0.0).astype(BF16)
-        moved = jnp.dot(picked, spread_ref[...], preferred_element_type=F32)
-        return jnp.where(same_bin, moved, 0.0).astype(BF16)
-
+        return jnp.broadcast_to(normed[None], (DIGIT, SLOT, OFFS)).reshape(size, OFFS)
+
+    picked = jnp.concatenate(
+        [jnp.where(same_digit, repeated(part), 0.0).astype(BF16) for part in (real, imag)], axis=0
+    )
+    moved = jnp.dot(picked, spread_ref[...], preferred_element_type=F32)
+    moved = jnp.concatenate(
+        [jnp.where(same_bin, moved[at * size : (at + 1) * size], 0.0) for at in range(2)], axis=0
+    ).astype(BF16)
     turns = turns_ref[...]
     fine = [jnp.concatenate(pair, axis=1).astype(BF16) for pair in powers_of(*turn_waves(turns))]
     of_both = jnp.dot(
-        jnp.concatenate([spread(real), spread(imag)], axis=0),
-        jnp.concatenate(fine, axis=0),
-        preferred_element_type=F32,
+        moved, jnp.concatenate(fine, axis=0), preferred_element_type=F32
     )
     along = jnp.zeros((SLOT, VEL), F32)
     across = jnp.zeros((SLOT, VEL), F32)

time: 52 us -> 51.9 us (level)
  Pallas kernels: 8.36 us -> 7.25 us
  waiting for transfers between devices: 6.72 us -> 7.76 us
    ppermute x1, waiting for transfers between devices: 6.72 us -> 7.76 us  [local(): lax.ppermute(received[:WIN_DEVICES], 'seg', [(s, s - 1) for s in range(1,...]
    pallas_call x1, Pallas kernels: 3.09 us -> 2.05 us  [own_products(): pl.pallas_call(own_kernel, out_shape=jax.ShapeDtypeStruct((TAKEN, 2 * WAV...]
  transfers between devices with their start and end apart: 2 -> 2, of which waited for: 1 -> 1; matrix products, arithmetic and copies ran while one was open for 0% -> 0% of each run, Pallas kernels for 6% -> 4%
where the time goes in v5:
time: 51.9 us; the launch traced here: 51.7 us
  blocking collectives  32.5 us (63%)
  waiting for transfers between devices  7.76 us (15%)
  Pallas kernels  7.25 us (14%)
  starting transfers between devices  2.85 us (5%)
  matrix products  0.88 us (2%)
    all_to_all x1, blocking collectives, exchange(): return lax.all_to_all(values, ('blk', 'win'), 0, 0, tiled=True)  23.4 us
    all_to_all x1, blocking collectives, local(): images = lax.all_to_all(images, 'blk', 0, 0, tiled=True)  9.12 us
    ppermute x1, waiting for transfers between devices, local(): lax.ppermute(received[:WIN_DEVICES], 'seg', [(s, s - 1) for s in range(1,...  7.76 us
    pallas_call x1, Pallas kernels, whiten(): pl.pallas_call(whiten_kernel, in_specs=[pl.BlockSpec(memory_space=pl.ANY)...  3.57 us
    ppermute x1, starting transfers between devices, local(): lax.ppermute(received[:WIN_DEVICES], 'seg', [(s, s - 1) for s in range(1,...  2.05 us
    pallas_call x1, Pallas kernels, own_products(): pl.pallas_call(own_kernel, out_shape=jax.ShapeDtypeStruct((TAKEN, 2 * WAV...  2.05 us
    pallas_call x1, Pallas kernels, image_of(): pl.pallas_call(image_kernel, out_shape=jax.ShapeDtypeStruct((SEG_BLOCKS,...  1.64 us
  transfers between devices with their start and end apart: 2, of which 1 were waited for; matrix products, arithmetic and copies ran while one was open for 0% of the time, Pallas kernels for 4%

profile of v5, /device:TPU:192, one launch (start us, length us, event | category | flops | bytes accessed | tf_op | source)
XLA Modules:
  0.0 51.7 jit_solution(16197549003088577192)
XLA Ops:
  0.0 3.6 %whiten.1 = bf16[32,104,128]{2,1,0:T(8,128)(2,1)S(1)} custom-call(bf16[2,2000,256]{2,1,0:T(8,128)(2,1)} %samples_hbm.1, bf16[4,832,256]{2,1,0:T(8,128)(2,1)} %constant.59.clone.table_hbm, f32[1,256]{1,0:T(1,128)} %bitcast.4), custom_call_target="tpu_custom_call" | custom-call | flops 1703936000 | bytes 5242880 | tf_op jit(solution)/shard_map/whiten/pallas_call | solution.py:266
  3.6 0.0 copy-start.4
  3.6 0.8 %collective-permute-start = (bf16[4,104,128]{2,1,0:T(8,128)(2,1)S(1)}, bf16[4,104,128]{2,1,0:T(8,128)(2,1)S(1)}, u32[]{:S(2)}, u32[]{:S(2)}) collective-permute-start(bf16[4,104,128]{2,1,0:T(8,128)(2,1)S(1)} %slice.17), channel_id=1, source_target_pairs={{256,224},{288,256},{320,288},{352,320},{384,352},{416,384},{448,4... | collective-permute-start | bytes 319496 | tf_op jit(solution)/shard_map/ppermute | solution.py:501
  4.5 0.1 copy-done.4
  4.6 23.4 %conditional.4 = (bf16[32,104,128]{2,1,0:T(8,128)(2,1)S(1)}, f32[32,1024]{1,0:T(8,128)S(1)}) conditional(s32[]{:T(128)} %convert_element_type.19, (bf16[32,104,128]{2,1,0:T(8,128)(2,1)S(1)}, bf16[256,1024]{1,0:T(8,128)(2,1)S(1)}) %tuple.37, (bf16[32,104,128]{2,1,0:T(8,128)(2,1)S(1)}, f32[32,1024]{1,0:T(8,128)S(1)}) %tuple.27), branch_computations={%region_2.0_spmd, %region_3.0_spmd} | conditional | flops 1073741824 | bytes 10092560 | solution.py:505
  4.6 23.4 %all_to_all.14 = bf16[32,104,128]{2,1,0:T(8,128)(2,1)S(1)} all-to-all(bf16[32,104,128]{2,1,0:T(8,128)(2,1)S(1)} %get-tuple-element.28), channel_id=1, replica_groups=mesh['seg'=16,'blk'=8,'win'=4] {'blk','win'}, dimensions={0} | all-to-all | bytes 1703936 | tf_op jit(solution)/shard_map/cond/branch_1_fun/all_to_all | solution.py:497
  28.0 0.0 collective-permute-done.behind_ref
  28.0 0.0 copy-start
  28.0 0.0 copy-start.1
  28.1 0.0 copy-start.2
  28.1 2.1 %collective-permute-start.1 = (bf16[4,104,128]{2,1,0:T(8,128)(2,1)S(1)}, bf16[4,104,128]{2,1,0:T(8,128)(2,1)S(1)}, u32[]{:S(2)}, u32[]{:S(2)}) collective-permute-start(bf16[4,104,128]{2,1,0:T(8,128)(2,1)S(1)} %get-tuple-element.45), channel_id=1, source_target_pairs={{32,0},{64,32},{96,64},{128,96},{160,128},{192,160},{224,192},{33,... | collective-permute-start | bytes 319496 | tf_op jit(solution)/shard_map/ppermute | solution.py:514
  30.1 0.1 broadcast_multiply_fusion.turns_ref
  30.2 2.0 %conditional.5 = (f32[32,1024]{1,0:T(8,128)S(1)}) conditional(s32[]{:T(128)} %convert_element_type.19, f32[32,1024]{1,0:T(8,128)S(1)} %get-tuple-element.42, (bf16[32,104,128]{2,1,0:T(8,128)(2,1)S(1)}, bf16[256,1024]{1,0:T(8,128)(2,1)S(1)}) %tuple.38), branch_computations={%region_4.0_spmd, %region_5.0_spmd} | conditional | flops 1073741824 | bytes 8388616 | solution.py:515
  30.2 2.0 %own_products.3 = f32[32,1024]{1,0:T(8,128)S(1)} custom-call(bf16[32,104,128]{2,1,0:T(8,128)(2,1)S(1)} %get-tuple-element.30.recv_ref, bf16[256,1024]{1,0:T(8,128)(2,1)S(1)} %get-tuple-element.31.table_ref), custom_call_target="tpu_custom_call" | custom-call | flops 1073741824 | bytes 8388608 | tf_op jit(solution)/shard_map/cond/branch_1_fun/own_products/pallas_call | solution.py:363
  32.3 0.0 copy-start.3
  32.3 7.8 %collective-permute-done.1.ahead_ref = bf16[4,104,128]{2,1,0:T(8,128)(2,1)S(1)} collective-permute-done((bf16[4,104,128]{2,1,0:T(8,128)(2,1)S(1)}, bf16[4,104,128]{2,1,0:T(8,128)(2,1)S(1)}, u32[]{:S(2)}, u32[]{:S(2)}) %collective-permute-start.1) | collective-permute-done | bytes 106528 | tf_op jit(solution)/shard_map/ppermute | solution.py:514
  40.0 0.0 copy-done
  40.0 0.0 copy-done.1
  40.0 0.0 copy-done.2
  40.0 1.6 %image.1 = f32[8,16,128]{2,1,0:T(8,128)S(1)} custom-call(bf16[4,104,128]{2,1,0:T(8,128)(2,1)S(1)} %collective-permute-done.1.ahead_ref, bf16[4,104,128]{2,1,0:T(8,128)(2,1)S(1)} %collective-permute-done.behind_ref, bf16[4,104,128]{2,1,0:T(8,128)(2,1)S(1)} %get-tuple-element.44.last_ref, bf16[256,1024]{1,0:T(8,128)(2,1)S(1)} %copy-done, ...), custom_call_target="tpu_custom_call" | custom-call | flops 734003200 | bytes 6291456 | tf_op jit(solution)/shard_map/image/pallas_call | solution.py:464
  41.7 9.1 %all_to_all.15 = f32[8,16,128]{2,1,0:T(8,128)S(1)} all-to-all(f32[8,16,128]{2,1,0:T(8,128)S(1)} %image.1), channel_id=1, replica_groups=mesh['seg'=16,'blk'=8,'win'=4] {'blk'}, dimensions={0} | all-to-all | bytes 131072 | tf_op jit(solution)/shard_map/all_to_all | solution.py:533
  50.8 0.0 copy-done.3
  50.8 0.9 %fusion = f32[64,100]{1,0:T(8,128)} fusion(f32[128,100]{1,0:T(8,128)S(1)} %copy-done.3, f32[128,128]{1,0:T(8,128)S(1)} %bitcast.3), kind=kOutput, calls=%fused_computation | convolution fusion | flops 9830400 | bytes 142336 | tf_op jit(solution)/shard_map/dot_general | solution.py:479
  (6 shorter events, 0.1 us)
Async XLA Ops:
  3.6 1.0 %copy-start.4 = (bf16[256,1024]{1,0:T(8,128)(2,1)S(1)}, bf16[256,1024]{1,0:T(8,128)(2,1)}, u32[]{:S(2)}) copy-start(bf16[256,1024]{1,0:T(8,128)(2,1)} %constant.60.clone) | copy-start | bytes 1572868
  3.6 24.4 %collective-permute-start = (bf16[4,104,128]{2,1,0:T(8,128)(2,1)S(1)}, bf16[4,104,128]{2,1,0:T(8,128)(2,1)S(1)}, u32[]{:S(2)}, u32[]{:S(2)}) collective-permute-start(bf16[4,104,128]{2,1,0:T(8,128)(2,1)S(1)} %slice.17), channel_id=1, source_target_pairs={{256,224},{288,256},{320,288},{352,320},{384,352},{416,384},{448,4... | collective-permute-start | bytes 319496 | tf_op jit(solution)/shard_map/ppermute | solution.py:501
  28.0 12.0 %copy-start = (bf16[256,1024]{1,0:T(8,128)(2,1)S(1)}, bf16[256,1024]{1,0:T(8,128)(2,1)}, u32[]{:S(2)}) copy-start(bf16[256,1024]{1,0:T(8,128)(2,1)} %constant.61.clone.table_ref) | copy-start | bytes 1572868
  28.0 12.0 %copy-start.1 = (bf16[512,512]{1,0:T(8,128)(2,1)S(1)}, bf16[512,512]{1,0:T(8,128)(2,1)}, u32[]{:S(2)}) copy-start(bf16[512,512]{1,0:T(8,128)(2,1)} %constant.62.clone.lead_ref) | copy-start | bytes 1572868
  28.1 12.0 %copy-start.2 = (bf16[256,256]{1,0:T(8,128)(2,1)S(1)}, bf16[256,256]{1,0:T(8,128)(2,1)}, u32[]{:S(2)}) copy-start(bf16[256,256]{1,0:T(8,128)(2,1)} %constant.63.clone.spread_ref) | copy-start | bytes 393220
  28.1 12.0 %collective-permute-start.1 = (bf16[4,104,128]{2,1,0:T(8,128)(2,1)S(1)}, bf16[4,104,128]{2,1,0:T(8,128)(2,1)S(1)}, u32[]{:S(2)}, u32[]{:S(2)}) collective-permute-start(bf16[4,104,128]{2,1,0:T(8,128)(2,1)S(1)} %get-tuple-element.45), channel_id=1, source_target_pairs={{32,0},{64,32},{96,64},{128,96},{160,128},{192,160},{224,192},{33,... | collective-permute-start | bytes 319496 | tf_op jit(solution)/shard_map/ppermute | solution.py:514
  32.3 18.5 %copy-start.3 = (f32[128,100]{1,0:T(8,128)S(1)}, f32[128,100]{1,0:T(8,128)}, u32[]{:S(2)}) copy-start(f32[128,100]{1,0:T(8,128)} %constant.64.clone) | copy-start | bytes 153604

commit v6 on v5

--- a/solution.py
+++ b/solution.py
@@ -138,11 +138,10 @@
 
 
 def powers_of(cosine, sine):
-    now = (jnp.ones_like(cosine), jnp.zeros_like(sine))
-    waves = [now]
-    for _ in range(DIGIT - 1):
-        now = (now[0] * cosine - now[1] * sine, now[1] * cosine + now[0] * sine)
-        waves.append(now)
+    waves = [(jnp.ones_like(cosine), jnp.zeros_like(sine)), (cosine, sine)]
+    for power in range(2, DIGIT):
+        one, two = waves[power // 2], waves[power - power // 2]
+        waves.append((one[0] * two[0] - one[1] * two[1], one[1] * two[0] + one[0] * two[1]))
     return waves
 
 

time: 51.9 us -> 51.9 us (level)
  no operation moved by 1% of the time
where the time goes in v6:
time: 51.9 us; the launch traced here: 51.7 us
  blocking collectives  32.5 us (63%)
  waiting for transfers between devices  7.76 us (15%)
  Pallas kernels  7.22 us (14%)
  starting transfers between devices  2.85 us (5%)
  matrix products  0.88 us (2%)
    all_to_all x1, blocking collectives, exchange(): return lax.all_to_all(values, ('blk', 'win'), 0, 0, tiled=True)  23.4 us
    all_to_all x1, blocking collectives, local(): images = lax.all_to_all(images, 'blk', 0, 0, tiled=True)  9.12 us
    ppermute x1, waiting for transfers between devices, local(): lax.ppermute(received[:WIN_DEVICES], 'seg', [(s, s - 1) for s in range(1,...  7.76 us
    pallas_call x1, Pallas kernels, whiten(): pl.pallas_call(whiten_kernel, in_specs=[pl.BlockSpec(memory_space=pl.ANY)...  3.57 us
    ppermute x1, starting transfers between devices, local(): lax.ppermute(received[:WIN_DEVICES], 'seg', [(s, s - 1) for s in range(1,...  2.05 us
    pallas_call x1, Pallas kernels, own_products(): pl.pallas_call(own_kernel, out_shape=jax.ShapeDtypeStruct((TAKEN, 2 * WAV...  2.05 us
    pallas_call x1, Pallas kernels, image_of(): pl.pallas_call(image_kernel, out_shape=jax.ShapeDtypeStruct((SEG_BLOCKS,...  1.61 us
  transfers between devices with their start and end apart: 2, of which 1 were waited for; matrix products, arithmetic and copies ran while one was open for 0% of the time, Pallas kernels for 4%

profile of v6, /device:TPU:192, one launch (start us, length us, event | category | flops | bytes accessed | tf_op | source)
XLA Modules:
  0.0 51.7 jit_solution(16498320371187499721)
XLA Ops:
  0.0 3.6 %whiten.1 = bf16[32,104,128]{2,1,0:T(8,128)(2,1)S(1)} custom-call(bf16[2,2000,256]{2,1,0:T(8,128)(2,1)} %samples_hbm.1, bf16[4,832,256]{2,1,0:T(8,128)(2,1)} %constant.59.clone.table_hbm, f32[1,256]{1,0:T(1,128)} %bitcast.4), custom_call_target="tpu_custom_call" | custom-call | flops 1703936000 | bytes 5242880 | tf_op jit(solution)/shard_map/whiten/pallas_call | solution.py:265
  3.6 0.0 copy-start.4
  3.6 0.8 %collective-permute-start = (bf16[4,104,128]{2,1,0:T(8,128)(2,1)S(1)}, bf16[4,104,128]{2,1,0:T(8,128)(2,1)S(1)}, u32[]{:S(2)}, u32[]{:S(2)}) collective-permute-start(bf16[4,104,128]{2,1,0:T(8,128)(2,1)S(1)} %slice.17), channel_id=1, source_target_pairs={{256,224},{288,256},{320,288},{352,320},{384,352},{416,384},{448,4... | collective-permute-start | bytes 319496 | tf_op jit(solution)/shard_map/ppermute | solution.py:500
  4.5 0.1 copy-done.4
  4.6 23.4 %conditional.4 = (bf16[32,104,128]{2,1,0:T(8,128)(2,1)S(1)}, f32[32,1024]{1,0:T(8,128)S(1)}) conditional(s32[]{:T(128)} %convert_element_type.19, (bf16[32,104,128]{2,1,0:T(8,128)(2,1)S(1)}, bf16[256,1024]{1,0:T(8,128)(2,1)S(1)}) %tuple.37, (bf16[32,104,128]{2,1,0:T(8,128)(2,1)S(1)}, f32[32,1024]{1,0:T(8,128)S(1)}) %tuple.27), branch_computations={%region_2.0_spmd, %region_3.0_spmd} | conditional | flops 1073741824 | bytes 10092560 | solution.py:504
  4.6 23.4 %all_to_all.14 = bf16[32,104,128]{2,1,0:T(8,128)(2,1)S(1)} all-to-all(bf16[32,104,128]{2,1,0:T(8,128)(2,1)S(1)} %get-tuple-element.28), channel_id=1, replica_groups=mesh['seg'=16,'blk'=8,'win'=4] {'blk','win'}, dimensions={0} | all-to-all | bytes 1703936 | tf_op jit(solution)/shard_map/cond/branch_1_fun/all_to_all | solution.py:496
  28.0 0.0 collective-permute-done.behind_ref
  28.0 0.0 copy-start
  28.0 0.0 copy-start.1
  28.1 0.0 copy-start.2
  28.1 2.1 %collective-permute-start.1 = (bf16[4,104,128]{2,1,0:T(8,128)(2,1)S(1)}, bf16[4,104,128]{2,1,0:T(8,128)(2,1)S(1)}, u32[]{:S(2)}, u32[]{:S(2)}) collective-permute-start(bf16[4,104,128]{2,1,0:T(8,128)(2,1)S(1)} %get-tuple-element.45), channel_id=1, source_target_pairs={{32,0},{64,32},{96,64},{128,96},{160,128},{192,160},{224,192},{33,... | collective-permute-start | bytes 319496 | tf_op jit(solution)/shard_map/ppermute | solution.py:513
  30.1 0.1 broadcast_multiply_fusion.turns_ref
  30.2 2.0 %conditional.5 = (f32[32,1024]{1,0:T(8,128)S(1)}) conditional(s32[]{:T(128)} %convert_element_type.19, f32[32,1024]{1,0:T(8,128)S(1)} %get-tuple-element.42, (bf16[32,104,128]{2,1,0:T(8,128)(2,1)S(1)}, bf16[256,1024]{1,0:T(8,128)(2,1)S(1)}) %tuple.38), branch_computations={%region_4.0_spmd, %region_5.0_spmd} | conditional | flops 1073741824 | bytes 8388616 | solution.py:514
  30.2 2.0 %own_products.3 = f32[32,1024]{1,0:T(8,128)S(1)} custom-call(bf16[32,104,128]{2,1,0:T(8,128)(2,1)S(1)} %get-tuple-element.30.recv_ref, bf16[256,1024]{1,0:T(8,128)(2,1)S(1)} %get-tuple-element.31.table_ref), custom_call_target="tpu_custom_call" | custom-call | flops 1073741824 | bytes 8388608 | tf_op jit(solution)/shard_map/cond/branch_1_fun/own_products/pallas_call | solution.py:362
  32.3 0.0 copy-start.3
  32.3 7.8 %collective-permute-done.1.ahead_ref = bf16[4,104,128]{2,1,0:T(8,128)(2,1)S(1)} collective-permute-done((bf16[4,104,128]{2,1,0:T(8,128)(2,1)S(1)}, bf16[4,104,128]{2,1,0:T(8,128)(2,1)S(1)}, u32[]{:S(2)}, u32[]{:S(2)}) %collective-permute-start.1) | collective-permute-done | bytes 106528 | tf_op jit(solution)/shard_map/ppermute | solution.py:513
  40.0 0.0 copy-done
  40.0 0.0 copy-done.1
  40.0 0.0 copy-done.2
  40.0 1.6 %image.1 = f32[8,16,128]{2,1,0:T(8,128)S(1)} custom-call(bf16[4,104,128]{2,1,0:T(8,128)(2,1)S(1)} %collective-permute-done.1.ahead_ref, bf16[4,104,128]{2,1,0:T(8,128)(2,1)S(1)} %collective-permute-done.behind_ref, bf16[4,104,128]{2,1,0:T(8,128)(2,1)S(1)} %get-tuple-element.44.last_ref, bf16[256,1024]{1,0:T(8,128)(2,1)S(1)} %copy-done, ...), custom_call_target="tpu_custom_call" | custom-call | flops 734003200 | bytes 6291456 | tf_op jit(solution)/shard_map/image/pallas_call | solution.py:463
  41.6 9.1 %all_to_all.15 = f32[8,16,128]{2,1,0:T(8,128)S(1)} all-to-all(f32[8,16,128]{2,1,0:T(8,128)S(1)} %image.1), channel_id=1, replica_groups=mesh['seg'=16,'blk'=8,'win'=4] {'blk'}, dimensions={0} | all-to-all | bytes 131072 | tf_op jit(solution)/shard_map/all_to_all | solution.py:532
  50.8 0.0 copy-done.3
  50.8 0.9 %fusion = f32[64,100]{1,0:T(8,128)} fusion(f32[128,100]{1,0:T(8,128)S(1)} %copy-done.3, f32[128,128]{1,0:T(8,128)S(1)} %bitcast.3), kind=kOutput, calls=%fused_computation | convolution fusion | flops 9830400 | bytes 142336 | tf_op jit(solution)/shard_map/dot_general | solution.py:478
  (6 shorter events, 0.1 us)
Async XLA Ops:
  3.6 1.0 %copy-start.4 = (bf16[256,1024]{1,0:T(8,128)(2,1)S(1)}, bf16[256,1024]{1,0:T(8,128)(2,1)}, u32[]{:S(2)}) copy-start(bf16[256,1024]{1,0:T(8,128)(2,1)} %constant.60.clone) | copy-start | bytes 1572868
  3.6 24.4 %collective-permute-start = (bf16[4,104,128]{2,1,0:T(8,128)(2,1)S(1)}, bf16[4,104,128]{2,1,0:T(8,128)(2,1)S(1)}, u32[]{:S(2)}, u32[]{:S(2)}) collective-permute-start(bf16[4,104,128]{2,1,0:T(8,128)(2,1)S(1)} %slice.17), channel_id=1, source_target_pairs={{256,224},{288,256},{320,288},{352,320},{384,352},{416,384},{448,4... | collective-permute-start | bytes 319496 | tf_op jit(solution)/shard_map/ppermute | solution.py:500
  28.0 12.0 %copy-start = (bf16[256,1024]{1,0:T(8,128)(2,1)S(1)}, bf16[256,1024]{1,0:T(8,128)(2,1)}, u32[]{:S(2)}) copy-start(bf16[256,1024]{1,0:T(8,128)(2,1)} %constant.61.clone.table_ref) | copy-start | bytes 1572868
  28.0 12.0 %copy-start.1 = (bf16[512,512]{1,0:T(8,128)(2,1)S(1)}, bf16[512,512]{1,0:T(8,128)(2,1)}, u32[]{:S(2)}) copy-start(bf16[512,512]{1,0:T(8,128)(2,1)} %constant.62.clone.lead_ref) | copy-start | bytes 1572868
  28.1 12.0 %copy-start.2 = (bf16[256,256]{1,0:T(8,128)(2,1)S(1)}, bf16[256,256]{1,0:T(8,128)(2,1)}, u32[]{:S(2)}) copy-start(bf16[256,256]{1,0:T(8,128)(2,1)} %constant.63.clone.spread_ref) | copy-start | bytes 393220
  28.1 12.0 %collective-permute-start.1 = (bf16[4,104,128]{2,1,0:T(8,128)(2,1)S(1)}, bf16[4,104,128]{2,1,0:T(8,128)(2,1)S(1)}, u32[]{:S(2)}, u32[]{:S(2)}) collective-permute-start(bf16[4,104,128]{2,1,0:T(8,128)(2,1)S(1)} %get-tuple-element.45), channel_id=1, source_target_pairs={{32,0},{64,32},{96,64},{128,96},{160,128},{192,160},{224,192},{33,... | collective-permute-start | bytes 319496 | tf_op jit(solution)/shard_map/ppermute | solution.py:513
  32.3 18.5 %copy-start.3 = (f32[128,100]{1,0:T(8,128)S(1)}, f32[128,100]{1,0:T(8,128)}, u32[]{:S(2)}) copy-start(f32[128,100]{1,0:T(8,128)} %constant.64.clone) | copy-start | bytes 153604
